TPU v7x, 32 devices: a whole 2x2x4 slice. The times are simulated.
32 devices in a mesh: wide: 4 (over y, x), narrow: 8 (over z, core).
Axes of the slice: x: 2, y: 2, z: 4, core: 2. Of those that a mesh axis runs over, the one named last changes fastest.
Arguments:
- x_in: bfloat16 [64, 640, 768], P(('wide', 'narrow'))
- cotangent: bfloat16 [64, 640, 768], P(('wide', 'narrow')), may hold values from -6 to 6
- segment_ids: int32 [64, 640], P(('wide', 'narrow')), may hold values from 0 to 7, never falling along the last dimension, each value on 1 to 320 neighbouring positions
- type_ids: int32 [64, 640], P(('wide', 'narrow')), may hold values 0 or 1
- projection: float32 [768, 4608], P('narrow'), may hold values from -0.21875 to 0.21875
- context_out: float32 [768, 768], P('narrow'), may hold values from -2 to 2
- expand_weight: float32 [768, 3072], P('narrow'), may hold values from -0.21875 to 0.21875
- reduce_weight: float32 [3072, 768], P('narrow'), may hold values from -0.109375 to 0.109375
- vector_params: float32 [15, 768], P(None, 'narrow')
- first_projection: float32 [768, 4608], P('narrow'), may hold values from -0.00048828125 to 0.00048828125
- first_context: float32 [768, 768], P('narrow'), may hold values from -0.00048828125 to 0.00048828125
- first_expand: float32 [768, 3072], P('narrow'), may hold values from -0.00048828125 to 0.00048828125
- first_reduce: float32 [3072, 768], P('narrow'), may hold values from -0.00048828125 to 0.00048828125
- first_vectors: float32 [15, 768], P(None, 'narrow'), may hold values from -0.0017089844 to 0.0017089844
- second_projection: float32 [768, 4608], P('narrow'), may hold values from 1.12881086e-10 to 4.5152435e-10
- second_context: float32 [768, 768], P('narrow'), may hold values from 2.2576217e-11 to 9.030487e-11
- second_expand: float32 [768, 3072], P('narrow'), may hold values from 1.12881086e-10 to 4.5152435e-10
- second_reduce: float32 [3072, 768], P('narrow'), may hold values from 1.12881086e-10 to 4.5152435e-10
- second_vectors: float32 [15, 768], P(None, 'narrow'), may hold values from 1.1288108e-09 to 4.5152433e-09
Outputs:
- block_out: bfloat16 [64, 640, 768], P(('wide', 'narrow'))
- input_grad: bfloat16 [64, 640, 768], P(('wide', 'narrow'))
- grad_norm: float32 [], replicated
- new_projection: float32 [768, 4608], P('narrow')
- new_context: float32 [768, 768], P('narrow')
- new_expand: float32 [768, 3072], P('narrow')
- new_reduce: float32 [3072, 768], P('narrow')
- new_vectors: float32 [15, 768], P(None, 'narrow')
- next_first_projection: float32 [768, 4608], P('narrow')
- next_first_context: float32 [768, 768], P('narrow')
- next_first_expand: float32 [768, 3072], P('narrow')
- next_first_reduce: float32 [3072, 768], P('narrow')
- next_first_vectors: float32 [15, 768], P(None, 'narrow')
- next_second_projection: float32 [768, 4608], P('narrow')
- next_second_context: float32 [768, 768], P('narrow')
- next_second_expand: float32 [768, 3072], P('narrow')
- next_second_reduce: float32 [3072, 768], P('narrow')
- next_second_vectors: float32 [15, 768], P(None, 'narrow')
- copy_projection: bfloat16 [768, 4608], P('narrow')
- copy_context: bfloat16 [768, 768], P('narrow')
- copy_expand: bfloat16 [768, 3072], P('narrow')
- copy_reduce: bfloat16 [3072, 768], P('narrow')
- copy_vectors: bfloat16 [15, 768], P(None, 'narrow')
Inputs may be any that keep to these rules, and one draw needn't show every extreme that they name: `segment_ids`: ids never fall along a sequence; each document holds 1 to 320 positions.
All inputs are finite; a program needn't handle non-finite values. No bound on the sum of `type_ids` on one device may be relied on, other than what follows from the above.
Results may differ from a plain program's by a relative error of at most 0.017.
Values may be sent and summed in bfloat16 or wider, within the bound.
A program may use at most 256 MiB of HBM per device.

v0:
```python
import jax
import jax.numpy as jnp
from jax import lax
from jax.sharding import PartitionSpec as P

HEAD = 64
STEP = 10


beta_one = 0.9
beta_two = 0.999
adam_eps = 1e-08
norm_eps = 1e-05
clip_limit = 1.0
rate_table = (0.03, 0.3, 0.03, 0.015, 0.4)
decay_table = (0.01, 0.01, 0.01, 0.01, 0.0)


def layer_forward(resid, gain_row, shift_row):
    center = resid - jnp.mean(resid, axis=-1, keepdims=True)
    inverse = lax.rsqrt(jnp.mean(center * center, axis=-1, keepdims=True) + norm_eps)
    normed = center * inverse
    return (normed * gain_row + shift_row, normed, inverse)


def layer_backward(grad_out, normed, inverse, gain_row):
    scaled = grad_out * gain_row
    return inverse * (
        scaled
        - jnp.mean(scaled, axis=-1, keepdims=True)
        - normed * jnp.mean(scaled * normed, axis=-1, keepdims=True)
    )


def score_block(to_words, to_ents, keys_all, word_keys, segment_row):
    score_scale = to_words.shape[2] ** (-0.5)
    score_w = (
        jnp.einsum("ihd,jhd->hij", to_words, keys_all, preferred_element_type=jnp.float32)
        * score_scale
    )
    score_e = (
        jnp.einsum("ihd,jhd->hij", to_ents, keys_all, preferred_element_type=jnp.float32)
        * score_scale
    )
    scores = jnp.where(word_keys[None, None, :], score_w, score_e)
    same_doc = segment_row[:, None] == segment_row[None, :]
    return jnp.where(same_doc[None], scores, -1e30)


def attend(pieces):
    to_words, to_ents, keys_all, values_all, word_keys, segment_row = pieces
    scores = score_block(to_words, to_ents, keys_all, word_keys, segment_row)
    row_top = jnp.max(scores, axis=-1, keepdims=True)
    exp_scores = jnp.exp(scores - row_top)
    row_total = jnp.sum(exp_scores, axis=-1, keepdims=True)
    prob_half = (exp_scores / row_total).astype(jnp.bfloat16)
    context = jnp.einsum("hij,jhd->ihd", prob_half, values_all, preferred_element_type=jnp.float32)
    return (context, (row_top + jnp.log(row_total))[..., 0])


def attend_back(pieces):
    to_words, to_ents, keys_all, values_all, word_keys, segment_row, log_total, grad_context = (
        pieces
    )
    score_scale = to_words.shape[2] ** (-0.5)
    scores = score_block(to_words, to_ents, keys_all, word_keys, segment_row)
    prob_full = jnp.exp(scores - log_total[..., None])
    prob_half = prob_full.astype(jnp.bfloat16)
    grad_probs = jnp.einsum(
        "ihd,jhd->hij", grad_context, values_all, preferred_element_type=jnp.float32
    )
    grad_values = jnp.einsum(
        "hij,ihd->jhd", prob_half, grad_context, preferred_element_type=jnp.float32
    )
    row_inner = jnp.sum(prob_full * grad_probs, axis=-1, keepdims=True)
    grad_scores = (prob_full * (grad_probs - row_inner)).astype(jnp.bfloat16)
    zero_block = jnp.zeros_like(grad_scores)
    key_words = word_keys[None, None, :]
    grad_sw = jnp.where(key_words, grad_scores, zero_block)
    grad_se = jnp.where(key_words, zero_block, grad_scores)
    grad_tw = (
        jnp.einsum("hij,jhd->ihd", grad_sw, keys_all, preferred_element_type=jnp.float32)
        * score_scale
    )
    grad_te = (
        jnp.einsum("hij,jhd->ihd", grad_se, keys_all, preferred_element_type=jnp.float32)
        * score_scale
    )
    grad_keys = (
        jnp.einsum("hij,ihd->jhd", grad_sw, to_words, preferred_element_type=jnp.float32)
        + jnp.einsum("hij,ihd->jhd", grad_se, to_ents, preferred_element_type=jnp.float32)
    ) * score_scale
    return (
        grad_tw.astype(jnp.bfloat16),
        grad_te.astype(jnp.bfloat16),
        grad_keys.astype(jnp.bfloat16),
        grad_values.astype(jnp.bfloat16),
    )


def column_sum(array_in):
    return jnp.sum(array_in.astype(jnp.float32), axis=0)


def adam_update(master, first_old, second_old, grad_shard, factor, index):
    clipped = grad_shard * factor
    new_first = beta_one * first_old + (1.0 - beta_one) * clipped
    new_second = beta_two * second_old + (1.0 - beta_two) * clipped * clipped
    direction = (
        new_first
        / (1.0 - beta_one**STEP)
        / (jnp.sqrt(new_second / (1.0 - beta_two**STEP)) + adam_eps)
    )
    new_weight = master - rate_table[index] * (direction + decay_table[index] * master)
    return (new_weight, new_first, new_second)


def body(
    x_in,
    cotangent,
    segment_ids,
    type_ids,
    projection,
    context_out,
    expand_weight,
    reduce_weight,
    vector_params,
    first_projection,
    first_context,
    first_expand,
    first_reduce,
    first_vectors,
    second_projection,
    second_context,
    second_expand,
    second_reduce,
    second_vectors,
):
    seq_count, seq_len, model_width = x_in.shape
    head_count = model_width // HEAD
    tok_rows = seq_count * seq_len
    proj_w, ctx_w, expand_w, reduce_w, vec_half = (
        lax.all_gather(projection.astype(jnp.bfloat16), "narrow", axis=0, tiled=True),
        lax.all_gather(context_out.astype(jnp.bfloat16), "narrow", axis=0, tiled=True),
        lax.all_gather(expand_weight.astype(jnp.bfloat16), "narrow", axis=0, tiled=True),
        lax.all_gather(reduce_weight.astype(jnp.bfloat16), "narrow", axis=0, tiled=True),
        lax.all_gather(vector_params.astype(jnp.bfloat16), "narrow", axis=1, tiled=True),
    )
    vec_rows = vec_half.astype(jnp.float32)

    def heads_of(array_in):
        return array_in.reshape(seq_count, seq_len, head_count, HEAD)

    hidden = x_in.reshape(tok_rows, model_width)
    word_rows = (type_ids == 0).reshape(tok_rows, 1)
    projected = jnp.dot(hidden, proj_w, preferred_element_type=jnp.float32)
    queries = projected[:, 0 : 4 * model_width] + vec_rows[0:4].reshape(1, 4 * model_width)
    to_words = jnp.where(
        word_rows, queries[:, 0:model_width], queries[:, 2 * model_width : 3 * model_width]
    ).astype(jnp.bfloat16)
    to_ents = jnp.where(
        word_rows,
        queries[:, model_width : 2 * model_width],
        queries[:, 3 * model_width : 4 * model_width],
    ).astype(jnp.bfloat16)
    keys_all = projected[:, 4 * model_width : 5 * model_width].astype(jnp.bfloat16)
    values_all = (projected[:, 5 * model_width : 6 * model_width] + vec_rows[4]).astype(
        jnp.bfloat16
    )
    word_keys = type_ids == 0
    context, log_total = lax.map(
        attend,
        (
            heads_of(to_words),
            heads_of(to_ents),
            heads_of(keys_all),
            heads_of(values_all),
            word_keys,
            segment_ids,
        ),
    )
    context_half = context.reshape(tok_rows, model_width).astype(jnp.bfloat16)
    attn_out = jnp.dot(context_half, ctx_w, preferred_element_type=jnp.float32) + vec_rows[5]
    normed_one, unit_one, inverse_one = layer_forward(
        hidden.astype(jnp.float32) + attn_out, vec_rows[6], vec_rows[7]
    )
    normed_half = normed_one.astype(jnp.bfloat16)
    inner_bias = vec_rows[11:].reshape(1, -1)
    pre_act = jnp.dot(normed_half, expand_w, preferred_element_type=jnp.float32) + inner_bias
    activated = jax.nn.gelu(pre_act, approximate=False).astype(jnp.bfloat16)
    branch = jnp.dot(activated, reduce_w, preferred_element_type=jnp.float32) + vec_rows[8]
    block_out, unit_two, inverse_two = layer_forward(normed_one + branch, vec_rows[9], vec_rows[10])
    proj_b, ctx_b, expand_b, reduce_b = (
        lax.all_gather(projection.astype(jnp.bfloat16), "narrow", axis=0, tiled=True),
        lax.all_gather(context_out.astype(jnp.bfloat16), "narrow", axis=0, tiled=True),
        lax.all_gather(expand_weight.astype(jnp.bfloat16), "narrow", axis=0, tiled=True),
        lax.all_gather(reduce_weight.astype(jnp.bfloat16), "narrow", axis=0, tiled=True),
    )
    pre_back = jnp.dot(normed_half, expand_b, preferred_element_type=jnp.float32) + inner_bias
    grad_out = cotangent.reshape(tok_rows, model_width).astype(jnp.float32)
    gain_two = jnp.sum(grad_out * unit_two, axis=0)
    shift_two = jnp.sum(grad_out, axis=0)
    grad_r2 = layer_backward(grad_out, unit_two, inverse_two, vec_rows[9])
    grad_branch = grad_r2.astype(jnp.bfloat16)
    grad_reduce = jnp.einsum(
        "nf,nd->fd", activated, grad_branch, preferred_element_type=jnp.float32
    )
    grad_act = jnp.einsum("nd,fd->nf", grad_branch, reduce_b, preferred_element_type=jnp.float32)
    gelu_value, gelu_pull = jax.vjp(lambda pre_in: jax.nn.gelu(pre_in, approximate=False), pre_back)
    grad_pre = gelu_pull(grad_act)[0].astype(jnp.bfloat16)
    grad_expand = jnp.einsum("nd,nf->df", normed_half, grad_pre, preferred_element_type=jnp.float32)
    grad_h1 = (
        jnp.einsum("nf,df->nd", grad_pre, expand_b, preferred_element_type=jnp.float32) + grad_r2
    )
    gain_one = jnp.sum(grad_h1 * unit_one, axis=0)
    shift_one = jnp.sum(grad_h1, axis=0)
    grad_r1 = layer_backward(grad_h1, unit_one, inverse_one, vec_rows[6])
    grad_attn = grad_r1.astype(jnp.bfloat16)
    grad_context_w = jnp.einsum(
        "nd,ne->de", context_half, grad_attn, preferred_element_type=jnp.float32
    )
    grad_context = jnp.einsum(
        "ne,de->nd", grad_attn, ctx_b, preferred_element_type=jnp.float32
    ).astype(jnp.bfloat16)
    grad_tw, grad_te, grad_keys, grad_values = lax.map(
        attend_back,
        (
            heads_of(to_words),
            heads_of(to_ents),
            heads_of(keys_all),
            heads_of(values_all),
            word_keys,
            segment_ids,
            log_total,
            heads_of(grad_context),
        ),
    )
    grad_tw = grad_tw.reshape(tok_rows, model_width)
    grad_te = grad_te.reshape(tok_rows, model_width)
    grad_keys = grad_keys.reshape(tok_rows, model_width)
    grad_values = grad_values.reshape(tok_rows, model_width)
    zero_rows = jnp.zeros_like(grad_tw)
    grad_ww = jnp.where(word_rows, grad_tw, zero_rows)
    grad_we = jnp.where(word_rows, grad_te, zero_rows)
    grad_ew = jnp.where(word_rows, zero_rows, grad_tw)
    grad_ee = jnp.where(word_rows, zero_rows, grad_te)
    grad_projected = jnp.concatenate(
        [grad_ww, grad_we, grad_ew, grad_ee, grad_keys, grad_values], axis=1
    )
    grad_proj_w = jnp.einsum(
        "nd,ne->de", hidden, grad_projected, preferred_element_type=jnp.float32
    )
    input_grad = grad_r1 + jnp.einsum(
        "ne,de->nd", grad_projected, proj_b, preferred_element_type=jnp.float32
    )
    vector_rows = jnp.stack(
        [
            column_sum(grad_ww),
            column_sum(grad_we),
            column_sum(grad_ew),
            column_sum(grad_ee),
            column_sum(grad_values),
            column_sum(grad_attn),
            gain_one,
            shift_one,
            column_sum(grad_branch),
            gain_two,
            shift_two,
        ]
    )
    grad_vectors = jnp.concatenate(
        [vector_rows, column_sum(grad_pre).reshape(-1, model_width)], axis=0
    )
    shards = (
        lax.psum_scatter(grad_proj_w, "narrow", scatter_dimension=0, tiled=True),
        lax.psum_scatter(grad_context_w, "narrow", scatter_dimension=0, tiled=True),
        lax.psum_scatter(grad_expand, "narrow", scatter_dimension=0, tiled=True),
        lax.psum_scatter(grad_reduce, "narrow", scatter_dimension=0, tiled=True),
        lax.psum_scatter(grad_vectors, "narrow", scatter_dimension=1, tiled=True),
    )
    masters = (projection, context_out, expand_weight, reduce_weight, vector_params)
    firsts = (first_projection, first_context, first_expand, first_reduce, first_vectors)
    seconds = (second_projection, second_context, second_expand, second_reduce, second_vectors)
    shards = (
        lax.psum(shards[0].astype(jnp.bfloat16), "wide").astype(jnp.float32),
        lax.psum(shards[1].astype(jnp.bfloat16), "wide").astype(jnp.float32),
        lax.psum(shards[2].astype(jnp.bfloat16), "wide").astype(jnp.float32),
        lax.psum(shards[3].astype(jnp.bfloat16), "wide").astype(jnp.float32),
        lax.psum(shards[4].astype(jnp.bfloat16), "wide").astype(jnp.float32),
    )
    local_squares = sum((jnp.sum(shard_item * shard_item) for shard_item in shards))
    total_squares = lax.psum(local_squares, "narrow")
    grad_norm = jnp.sqrt(total_squares)
    factor = jnp.minimum(1.0, clip_limit / (grad_norm + 1e-06))
    results = [
        adam_update(masters[index], firsts[index], seconds[index], shards[index], factor, index)
        for index in range(5)
    ]
    out_shape = (seq_count, seq_len, model_width)
    return (
        block_out.astype(jnp.bfloat16).reshape(out_shape),
        input_grad.astype(jnp.bfloat16).reshape(out_shape),
        grad_norm,
        results[0][0],
        results[1][0],
        results[2][0],
        results[3][0],
        results[4][0],
        results[0][1],
        results[1][1],
        results[2][1],
        results[3][1],
        results[4][1],
        results[0][2],
        results[1][2],
        results[2][2],
        results[3][2],
        results[4][2],
        results[0][0].astype(jnp.bfloat16),
        results[1][0].astype(jnp.bfloat16),
        results[2][0].astype(jnp.bfloat16),
        results[3][0].astype(jnp.bfloat16),
        results[4][0].astype(jnp.bfloat16),
    )


def solution(mesh):
    return jax.shard_map(
        body,
        mesh=mesh,
        in_specs=(
            P(("wide", "narrow"), None, None),
            P(("wide", "narrow"), None, None),
            P(("wide", "narrow"), None),
            P(("wide", "narrow"), None),
            P("narrow", None),
            P("narrow", None),
            P("narrow", None),
            P("narrow", None),
            P(None, "narrow"),
            P("narrow", None),
            P("narrow", None),
            P("narrow", None),
            P("narrow", None),
            P(None, "narrow"),
            P("narrow", None),
            P("narrow", None),
            P("narrow", None),
            P("narrow", None),
            P(None, "narrow"),
        ),
        out_specs=(
            P(("wide", "narrow"), None, None),
            P(("wide", "narrow"), None, None),
            P(),
            P("narrow", None),
            P("narrow", None),
            P("narrow", None),
            P("narrow", None),
            P(None, "narrow"),
            P("narrow", None),
            P("narrow", None),
            P("narrow", None),
            P("narrow", None),
            P(None, "narrow"),
            P("narrow", None),
            P("narrow", None),
            P("narrow", None),
            P("narrow", None),
            P(None, "narrow"),
            P("narrow", None),
            P("narrow", None),
            P("narrow", None),
            P("narrow", None),
            P(None, "narrow"),
        ),
        check_vma=False,
    )
```

profile of v0, /device:TPU:0, one launch (start us, length us, event | category | flops | bytes accessed | tf_op | source)
XLA Modules:
  0.0 1059.4 jit_solution(15504883597518259294)
XLA Ops:
  15.0 15.8 %all-gather = bf16[8,96,15]{1,2,0:T(8,128)(2,1)S(1)} all-gather(bf16[1,96,15]{1,2,0:T(8,128)(2,1)S(1)} %convert_bitcast_fusion), channel_id=1, replica_groups=mesh['wide'=4,'narrow'=8] {'narrow'}, dimensions={0}, use_global_device_ids=true | all-gather | bytes 25920 | tf_op jit(solution)/shard_map/all_gather | solution.py:147
  34.2 50.2 %all-gather.6.cloned.1.call-done = bf16[768,4608]{1,0:T(8,128)(2,1)} async-done(((bf16[96,4608]{1,0:T(8,128)(2,1)}), bf16[768,4608]{1,0:T(8,128)(2,1)}) %all-gather.6.cloned.1.call-update) | async-done | bytes 7077904 | tf_op jit(solution)/shard_map/all_gather | solution.py:143
  84.3 17.3 %fusion.299 = f32[1280,4608]{1,0:T(8,128)} fusion(bf16[1280,768]{1,0:T(8,128)(2,1)} %bitcast.330, bf16[768,4608]{1,0:T(8,128)(2,1)} %all-gather.6.cloned.1.call-done), kind=kOutput, calls=%fused_computation.254 | convolution fusion | flops 9059696640 | bytes 32636928 | tf_op jit(solution)/shard_map/dot_general | solution.py:156
  101.6 3.6 slice.103
  105.2 6.6 slice_add_fusion
  113.9 4.0 copy.157
  117.9 5.0 reshape.275
  122.8 3.3 copy.161
  128.4 3.9 reshape.277
  138.6 5.0 reshape.274
  149.0 4.8 reshape.276
  155.7 92.6 %while.30 = (s32[]{:T(128)}, bf16[2,640,12,64]{1,3,2,0:T(8,128)(2,1)}, f32[2,12,640]{2,1,0:T(8,128)S(1)}, bf16[2,640,12,64]{1,3,2,0:T(8,128)(2,1)}, s32[2,640]{1...) while((s32[]{:T(128)}, ...), condition=%wide.region_3.4_spmd.clone, body=%wide.region_0.3_spmd.sunk.clone | while | flops 1936990720 | bytes 114158464 | solution.py:171
  156.2 10.8 %fusion.415 = f32[12,640,640]{1,2,0:T(8,128)} fusion(bf16[2,640,12,64]{1,3,2,0:T(8,128)(2,1)} %get-tuple-element.651, s32[]{:T(128)} %get-tuple-element.636, bf16[2,640,12,64]{1,3,2,0:T(8,128)(2,1)S(1)} %get-tuple-element.652), kind=kOutput, calls=%fused_computation.8.clone.1.clone | convolution fusion | flops 629145600 | bytes 21627904 | tf_op jit(solution)/shard_map/while/body/eval_jaxpr/ihd,jhd->hij/dot_general | solution.py:38
  167.3 14.3 %fusion.416 = (f32[12,640]{1,0:T(8,128)S(1)}, f32[12,640,640]{1,2,0:T(8,128)}) fusion(bf16[2,640,12,64]{1,3,2,0:T(8,128)(2,1)S(1)} %get-tuple-element.652, s32[]{:T(128)} %get-tuple-element.636, bf16[2,640,12,64]{1,3,2,0:T(8,128)(2,1)S(1)} %copy-done.2, f32[12,640,640]{1,2,0:T(8,128)} %fusion.415, ...), kind=kOutput, calls=%fused_computation.250.clone.1.clone | convolution fusion | flops 653713920 | bytes 41730048 | tf_op jit(solution)/shard_map/while/body/eval_jaxpr/ihd,jhd->hij/dot_general | solution.py:42
  181.6 9.4 fusion.417
  191.0 11.7 %bitcast_dynamic-update-slice_fusion.6 = bf16[2,640,12,64]{1,3,2,0:T(8,128)(2,1)} fusion(bf16[2,640,12,64]{1,3,2,0:T(8,128)(2,1)} %get-tuple-element.637, s32[]{:T(128)} %get-tuple-element.636, f32[12,640,640]{1,2,0:T(8,128)} %get-tuple-element.587, f32[12,640]{1,0:T(8,128)S(1)} %fusion.417, f32[12,640]{1,0:T(8,128)S(1)} %get-tuple-element.588, ...), kind=kOutput, calls=%fused_computation.5.clone.1.clone | convolution fusion | flops 643891200 | bytes 22672384 | tf_op jit(solution)/shard_map/while/body/eval_jaxpr/hij,jhd->ihd/dot_general | solution.py:57
  202.7 10.8 %fusion.415 = f32[12,640,640]{1,2,0:T(8,128)} fusion(bf16[2,640,12,64]{1,3,2,0:T(8,128)(2,1)} %get-tuple-element.651, s32[]{:T(128)} %get-tuple-element.636, bf16[2,640,12,64]{1,3,2,0:T(8,128)(2,1)S(1)} %get-tuple-element.652), kind=kOutput, calls=%fused_computation.8.clone.1.clone | convolution fusion | flops 629145600 | bytes 21627904 | tf_op jit(solution)/shard_map/while/body/eval_jaxpr/ihd,jhd->hij/dot_general | solution.py:38
  213.9 13.6 %fusion.416 = (f32[12,640]{1,0:T(8,128)S(1)}, f32[12,640,640]{1,2,0:T(8,128)}) fusion(bf16[2,640,12,64]{1,3,2,0:T(8,128)(2,1)S(1)} %get-tuple-element.652, s32[]{:T(128)} %get-tuple-element.636, bf16[2,640,12,64]{1,3,2,0:T(8,128)(2,1)S(1)} %copy-done.2, f32[12,640,640]{1,2,0:T(8,128)} %fusion.415, ...), kind=kOutput, calls=%fused_computation.250.clone.1.clone | convolution fusion | flops 653713920 | bytes 41730048 | tf_op jit(solution)/shard_map/while/body/eval_jaxpr/ihd,jhd->hij/dot_general | solution.py:42
  227.5 9.2 fusion.417
  236.7 11.5 %bitcast_dynamic-update-slice_fusion.6 = bf16[2,640,12,64]{1,3,2,0:T(8,128)(2,1)} fusion(bf16[2,640,12,64]{1,3,2,0:T(8,128)(2,1)} %get-tuple-element.637, s32[]{:T(128)} %get-tuple-element.636, f32[12,640,640]{1,2,0:T(8,128)} %get-tuple-element.587, f32[12,640]{1,0:T(8,128)S(1)} %fusion.417, f32[12,640]{1,0:T(8,128)S(1)} %get-tuple-element.588, ...), kind=kOutput, calls=%fused_computation.5.clone.1.clone | convolution fusion | flops 643891200 | bytes 22672384 | tf_op jit(solution)/shard_map/while/body/eval_jaxpr/hij,jhd->ihd/dot_general | solution.py:57
  248.4 4.3 copy.164
  254.4 4.5 fusion.297
  261.5 46.1 %multiply_convert_fusion.4 = (bf16[1280,3072]{1,0:T(8,128)(2,1)}, f32[1280,3072]{1,0:T(8,128)}, f32[1280,3072]{1,0:T(8,128)}) fusion(f32[3072]{0:T(1024)S(1)} %copy-done.48, bf16[768,3072]{1,0:T(8,128)(2,1)} %all-gather.10.cloned.1.call-done, f32[1280,768]{1,0:T(8,128)} %copy-done.7, f32[768]{0:T(1024)S(1)} %copy-done.50, f32[768]{0:T(1024)S(1)} %copy-done.41, ...), kind=kOutput, calls=%fused_computation.116 | convolution fusion | flops 6304235520 | bytes 48001024 | tf_op jit(solution)/shard_map/dot_general | solution.py:189
  307.7 11.1 %fusion.298 = (f32[1280]{0:T(1024)S(1)}, f32[1280,768]{1,0:T(8,128)S(1)}) fusion(f32[768]{0:T(1024)S(1)} %copy-done.51, bf16[1280,3072]{1,0:T(8,128)(2,1)} %get-tuple-element.420, bf16[3072,768]{1,0:T(8,128)(2,1)} %all-gather.12.cloned.1.call-done, f32[768]{0:T(1024)S(1)} %copy-done.50, f32[768]{0:T(1024)S(1)} %copy-done.41, ...), kind=kOutput, calls=%fused_computation.253 | convolution fusion | flops 6046678016 | bytes 20471808 | tf_op jit(solution)/shard_map/dot_general | solution.py:191
  323.1 4.1 convert_reduce_fusion.2
  327.2 23.8 %convert_reduce_fusion = (f32[3072]{0:T(1024)}, bf16[1280,3072]{1,0:T(8,128)(2,1)}) fusion(f32[1280,3072]{1,0:T(8,128)} %get-tuple-element.421, bf16[3072,768]{1,0:T(8,128)(2,1)} %all-gather.12.cloned.1.call-done, f32[1280,768]{1,0:T(8,128)} %get-tuple-element.417, f32[1280,3072]{1,0:T(8,128)} %get-tuple-element.431, f32[3072]{0:T(1024)S(1)} %copy-done.48), kind=kOutput, calls=%fused_computation.114 | convolution fusion | flops 6107624448 | bytes 47996928 | tf_op jit(solution)/shard_map/nd,fd->nf/dot_general | solution.py:208
  351.0 13.4 %multiply_reduce_fusion.1 = (f32[768]{0:T(1024)}, f32[1280]{0:T(1024)S(1)}, f32[1280]{0:T(1024)S(1)}, f32[768]{0:T(1024)}, f32[1280,768]{1,0:T(8,128)S(1)}) fusion(f32[1280,768]{1,0:T(8,128)} %copy-done.7, f32[1280]{0:T(1024)S(1)} %add_rsqrt_fusion.1, f32[1280]{0:T(1024)S(1)} %broadcast_multiply_fusion.4, f32[768]{0:T(1024)S(1)} %copy-done.41, ...), kind=kOutput, calls=%fused_computation.151 | convolution fusion | flops 6049624064 | bytes 24409088 | tf_op jit(solution)/shard_map/nf,df->nd/dot_general | solution.py:213
  371.6 12.9 %fusion.274 = f32[768,3072]{1,0:T(8,128)} fusion(bf16[1280,3072]{1,0:T(8,128)(2,1)} %get-tuple-element.436, f32[1280,768]{1,0:T(8,128)} %copy-done.7, f32[768]{0:T(1024)S(1)} %copy-done.50, f32[768]{0:T(1024)S(1)} %copy-done.41, f32[1280]{0:T(1024)S(1)} %add_rsqrt_fusion.1, f32[1280]{0:T(1024)S(1)} %broadcast_multiply_fusion.4), kind=kOutput, calls=%fused_computation.243 | convolution fusion | flops 6044712960 | bytes 21250048 | tf_op jit(solution)/shard_map/nd,nf->df/dot_general | solution.py:211
  384.6 12.1 %fusion.271 = f32[3072,768]{1,0:T(8,128)} fusion(bf16[1280,3072]{1,0:T(8,128)(2,1)} %get-tuple-element.420, f32[1280,768]{1,0:T(8,128)} %get-tuple-element.417), kind=kOutput, calls=%fused_computation.240 | convolution fusion | flops 6040780800 | bytes 21233664 | tf_op jit(solution)/shard_map/nf,nd->fd/dot_general | solution.py:205
  398.0 3.9 convolution_convert_fusion
  404.1 5.0 reshape.279
  412.4 241.8 %while.31 = (s32[]{:T(128)}, bf16[2,640,12,64]{1,3,2,0:T(8,128)(2,1)}, bf16[2,640,12,64]{1,3,2,0:T(8,128)(2,1)}, bf16[2,640,12,64]{1,3,2,0:T(8,128)(2,1)}, bf16[...) while((s32[]{:T(128)}, ...), condition=%wide.region_14.15_spmd.clone, body=%wide.region_12.14_spmd.sunk.clone | while | flops 9569353728 | bytes 277184160 | solution.py:225
  412.8 11.1 %fusion.452 = f32[12,640,640]{1,2,0:T(8,128)} fusion(bf16[2,640,12,64]{1,3,2,0:T(8,128)(2,1)} %get-tuple-element.688, s32[]{:T(128)} %get-tuple-element.667, bf16[2,640,12,64]{1,3,2,0:T(8,128)(2,1)S(1)} %get-tuple-element.685), kind=kOutput, calls=%fused_computation.65.clone.1.clone | convolution fusion | flops 629145600 | bytes 21627904 | tf_op jit(solution)/shard_map/while/body/eval_jaxpr/ihd,jhd->hij/dot_general | solution.py:38
  424.3 14.8 %subtract_exponential_fusion.4 = f32[12,640,640]{1,2,0:T(8,128)} fusion(f32[12,640,640]{1,2,0:T(8,128)} %fusion.452, f32[12,640]{1,0:T(8,128)S(1)} %dynamic-slice_bitcast_fusion.3, pred[640]{0:T(1024)(128)(4,1)S(1)} %dynamic-slice_reduce_fusion.11, pred[640,640]{0,1:T(8,128)(4,1)S(1)} %broadcast_compare_fusion.8, ...), kind=kOutput, calls=%fused_computation.28.clone.1.clone | convolution fusion | flops 653721600 | bytes 41740288 | tf_op jit(solution)/shard_map/while/body/eval_jaxpr/ihd,jhd->hij/dot_general | solution.py:42
  439.1 21.6 %fusion.456 = f32[12,64,640]{2,1,0:T(8,128)} fusion(pred[640]{0:T(1024)(128)(4,1)S(1)} %dynamic-slice_reduce_fusion.11, f32[12,640,640]{1,2,0:T(8,128)} %subtract_exponential_fusion.4, bf16[2,640,12,64]{1,3,2,0:T(8,128)(2,1)} %get-tuple-element.688, s32[]{:T(128)} %get-tuple-element.667, bf16[2,640,12,64]{1,3,2,0:T(8,128)(2,1)} %get-tuple-element.692, ...), kind=kOutput, calls=%fused_computation.34.clone.1.clone | convolution fusion | flops 1912021120 | bytes 46206080 | tf_op jit(solution)/shard_map/while/body/eval_jaxpr/hij,ihd->jhd/dot_general | solution.py:90
  460.7 21.6 %fusion.457 = bf16[2,640,12,64]{1,3,2,0:T(8,128)(2,1)} fusion(bf16[2,640,12,64]{1,3,2,0:T(8,128)(2,1)} %get-tuple-element.670, s32[]{:T(128)} %get-tuple-element.667, f32[12,64,640]{2,1,0:T(8,128)} %fusion.456, pred[640]{0:T(1024)(128)(4,1)S(1)} %dynamic-slice_reduce_fusion.11, f32[12,640,640]{1,2,0:T(8,128)} %subtract_exponential_fusion.4, ...), kind=kOutput, calls=%fused_computation.49.clone.1.clone | convolution fusion | flops 1913495680 | bytes 47189632 | tf_op jit(solution)/shard_map/while/body/eval_jaxpr/hij,ihd->jhd/dot_general | solution.py:91
  482.3 20.1 %fusion.455 = bf16[2,640,12,64]{1,3,2,0:T(8,128)(2,1)} fusion(bf16[2,640,12,64]{1,3,2,0:T(8,128)(2,1)} %get-tuple-element.669, s32[]{:T(128)} %get-tuple-element.667, pred[640]{0:T(1024)(128)(4,1)S(1)} %dynamic-slice_reduce_fusion.11, f32[12,640,640]{1,2,0:T(8,128)} %subtract_exponential_fusion.4, ...), kind=kOutput, calls=%fused_computation.47.clone.1.clone | convolution fusion | flops 1913004160 | bytes 45223936 | tf_op jit(solution)/shard_map/while/body/eval_jaxpr/hij,jhd->ihd/dot_general | solution.py:86
  502.4 11.4 %fusion.458 = bf16[2,640,12,64]{1,3,2,0:T(8,128)(2,1)} fusion(bf16[2,640,12,64]{1,3,2,0:T(8,128)(2,1)} %get-tuple-element.671, s32[]{:T(128)} %get-tuple-element.667, f32[12,640,640]{1,2,0:T(8,128)} %subtract_exponential_fusion.4, bf16[2,640,12,64]{1,3,2,0:T(8,128)(2,1)} %get-tuple-element.691), kind=kOutput, calls=%fused_computation.43.clone.1.clone | convolution fusion | flops 634552320 | bytes 21627904 | tf_op jit(solution)/shard_map/while/body/eval_jaxpr/hij,ihd->jhd/dot_general | solution.py:72
  513.7 20.0 %fusion.454 = bf16[2,640,12,64]{1,3,2,0:T(8,128)(2,1)} fusion(bf16[2,640,12,64]{1,3,2,0:T(8,128)(2,1)} %get-tuple-element.668, s32[]{:T(128)} %get-tuple-element.667, pred[640]{0:T(1024)(128)(4,1)S(1)} %dynamic-slice_reduce_fusion.11, f32[12,640,640]{1,2,0:T(8,128)} %subtract_exponential_fusion.4, ...), kind=kOutput, calls=%fused_computation.45.clone.1.clone | convolution fusion | flops 1913004160 | bytes 45223936 | tf_op jit(solution)/shard_map/while/body/eval_jaxpr/hij,jhd->ihd/dot_general | solution.py:82
  533.8 10.9 %fusion.452 = f32[12,640,640]{1,2,0:T(8,128)} fusion(bf16[2,640,12,64]{1,3,2,0:T(8,128)(2,1)} %get-tuple-element.688, s32[]{:T(128)} %get-tuple-element.667, bf16[2,640,12,64]{1,3,2,0:T(8,128)(2,1)S(1)} %get-tuple-element.685), kind=kOutput, calls=%fused_computation.65.clone.1.clone | convolution fusion | flops 629145600 | bytes 21627904 | tf_op jit(solution)/shard_map/while/body/eval_jaxpr/ihd,jhd->hij/dot_general | solution.py:38
  545.0 14.8 %subtract_exponential_fusion.4 = f32[12,640,640]{1,2,0:T(8,128)} fusion(f32[12,640,640]{1,2,0:T(8,128)} %fusion.452, f32[12,640]{1,0:T(8,128)S(1)} %dynamic-slice_bitcast_fusion.3, pred[640]{0:T(1024)(128)(4,1)S(1)} %dynamic-slice_reduce_fusion.11, pred[640,640]{0,1:T(8,128)(4,1)S(1)} %broadcast_compare_fusion.8, ...), kind=kOutput, calls=%fused_computation.28.clone.1.clone | convolution fusion | flops 653721600 | bytes 41740288 | tf_op jit(solution)/shard_map/while/body/eval_jaxpr/ihd,jhd->hij/dot_general | solution.py:42
  559.8 21.6 %fusion.456 = f32[12,64,640]{2,1,0:T(8,128)} fusion(pred[640]{0:T(1024)(128)(4,1)S(1)} %dynamic-slice_reduce_fusion.11, f32[12,640,640]{1,2,0:T(8,128)} %subtract_exponential_fusion.4, bf16[2,640,12,64]{1,3,2,0:T(8,128)(2,1)} %get-tuple-element.688, s32[]{:T(128)} %get-tuple-element.667, bf16[2,640,12,64]{1,3,2,0:T(8,128)(2,1)} %get-tuple-element.692, ...), kind=kOutput, calls=%fused_computation.34.clone.1.clone | convolution fusion | flops 1912021120 | bytes 46206080 | tf_op jit(solution)/shard_map/while/body/eval_jaxpr/hij,ihd->jhd/dot_general | solution.py:90
  581.4 21.5 %fusion.457 = bf16[2,640,12,64]{1,3,2,0:T(8,128)(2,1)} fusion(bf16[2,640,12,64]{1,3,2,0:T(8,128)(2,1)} %get-tuple-element.670, s32[]{:T(128)} %get-tuple-element.667, f32[12,64,640]{2,1,0:T(8,128)} %fusion.456, pred[640]{0:T(1024)(128)(4,1)S(1)} %dynamic-slice_reduce_fusion.11, f32[12,640,640]{1,2,0:T(8,128)} %subtract_exponential_fusion.4, ...), kind=kOutput, calls=%fused_computation.49.clone.1.clone | convolution fusion | flops 1913495680 | bytes 47189632 | tf_op jit(solution)/shard_map/while/body/eval_jaxpr/hij,ihd->jhd/dot_general | solution.py:91
  602.9 20.0 %fusion.455 = bf16[2,640,12,64]{1,3,2,0:T(8,128)(2,1)} fusion(bf16[2,640,12,64]{1,3,2,0:T(8,128)(2,1)} %get-tuple-element.669, s32[]{:T(128)} %get-tuple-element.667, pred[640]{0:T(1024)(128)(4,1)S(1)} %dynamic-slice_reduce_fusion.11, f32[12,640,640]{1,2,0:T(8,128)} %subtract_exponential_fusion.4, ...), kind=kOutput, calls=%fused_computation.47.clone.1.clone | convolution fusion | flops 1913004160 | bytes 45223936 | tf_op jit(solution)/shard_map/while/body/eval_jaxpr/hij,jhd->ihd/dot_general | solution.py:86
  622.9 11.1 %fusion.458 = bf16[2,640,12,64]{1,3,2,0:T(8,128)(2,1)} fusion(bf16[2,640,12,64]{1,3,2,0:T(8,128)(2,1)} %get-tuple-element.671, s32[]{:T(128)} %get-tuple-element.667, f32[12,640,640]{1,2,0:T(8,128)} %subtract_exponential_fusion.4, bf16[2,640,12,64]{1,3,2,0:T(8,128)(2,1)} %get-tuple-element.691), kind=kOutput, calls=%fused_computation.43.clone.1.clone | convolution fusion | flops 634552320 | bytes 21627904 | tf_op jit(solution)/shard_map/while/body/eval_jaxpr/hij,ihd->jhd/dot_general | solution.py:72
  634.0 20.0 %fusion.454 = bf16[2,640,12,64]{1,3,2,0:T(8,128)(2,1)} fusion(bf16[2,640,12,64]{1,3,2,0:T(8,128)(2,1)} %get-tuple-element.668, s32[]{:T(128)} %get-tuple-element.667, pred[640]{0:T(1024)(128)(4,1)S(1)} %dynamic-slice_reduce_fusion.11, f32[12,640,640]{1,2,0:T(8,128)} %subtract_exponential_fusion.4, ...), kind=kOutput, calls=%fused_computation.45.clone.1.clone | convolution fusion | flops 1913004160 | bytes 45223936 | tf_op jit(solution)/shard_map/while/body/eval_jaxpr/hij,jhd->ihd/dot_general | solution.py:82
  654.2 3.6 copy.171
  662.1 3.6 copy.173
  667.3 4.0 copy.174
  671.3 3.6 copy.177
  676.5 4.0 copy.179
  680.5 3.6 copy.178
  685.8 4.2 copy.180
  694.4 4.3 copy-done.29
  698.6 12.1 %convolution_bitcast_fusion = f32[768,4608]{0,1:T(8,128)} fusion(bf16[1280,4608]{1,0:T(8,128)(2,1)S(1)} %constant_dynamic-update-slice_fusion, bf16[1280,768]{1,0:T(8,128)(2,1)S(1)} %bitcast.332), kind=kOutput, calls=%fused_computation.130 | convolution fusion | flops 9059696640 | bytes 27918336 | tf_op jit(solution)/shard_map/nd,ne->de/dot_general | solution.py:250
  710.8 15.1 %copy.195 = f32[768,4608]{1,0:T(8,128)} copy(f32[768,4608]{0,1:T(8,128)} %convolution_bitcast_fusion) | data formatting | bytes 28311552
  740.4 127.9 %reduce-scatter.16.cloned.1.call-done = f32[96,4608]{1,0:T(8,128)} async-done(((f32[768,4608]{1,0:T(8,128)}), f32[96,4608]{1,0:T(8,128)}) %reduce-scatter.16.cloned.1.call-update) | async-done | bytes 1769488
  878.8 21.5 %reduce-scatter.18.cloned.1.call-done = f32[96,15]{1,0:T(8,128)} async-done(((f32[768,15]{1,0:T(8,128)}), f32[96,15]{1,0:T(8,128)}) %reduce-scatter.18.cloned.1.call-update) | async-done | bytes 5776
  901.1 9.8 psum.46
  911.5 68.4 %all-reduce.3.cloned.1.call-done = (bf16[96,4608]{0,1:T(8,128)(2,1)}, bf16[96,768]{1,0:T(8,128)(2,1)}, bf16[96,3072]{1,0:T(8,128)(2,1)}, bf16[384,768]{1,0:T(8,128)(2,1)}) async-done(((bf16[96,4608]{0,1:T(8,128)(2,1)}, bf16[96,768]{1,0:T(8,128)(2,1)}, bf16[96,3072]{1,0:T(8,128)(2,1)}, bf16[384,768]{1,0:T(8,128)(2,1)}), (bf16[96,4608]{0,1:T(8,128)(2,1)}, bf16[96,768]{1,0:T(8,128)(2,1)}, ...) | async-done | bytes 2211856 | tf_op jit(solution)/shard_map/psum | solution.py:285
  991.2 16.1 %fusion.247 = bf16[1280,768]{1,0:T(8,128)(2,1)} fusion(f32[1280,768]{1,0:T(8,128)} %copy-done.18, bf16[1280,4608]{1,0:T(8,128)(2,1)} %copy-done.29, bf16[768,4608]{1,0:T(8,128)(2,1)} %all-gather.6.cloned.1.call-done), kind=kOutput, calls=%fused_computation.173 | convolution fusion | flops 9061662720 | bytes 24772608 | tf_op jit(solution)/shard_map/ne,de->nd/dot_general | solution.py:253
  1007.3 16.8 %psum.47 = f32[]{:T(128)} all-reduce(f32[]{:T(128)S(6)} %add.269), channel_id=1, replica_groups=mesh['wide'=4,'narrow'=8] {'narrow'}, use_global_device_ids=true, to_apply=%region_42.43 | all-reduce | flops 1 | bytes 8 | tf_op jit(solution)/shard_map/psum | solution.py:292
  1024.9 7.0 fusion.290
  1042.5 4.9 fusion.281
  (250 shorter events, 115.0 us)
Async XLA Ops:
  7.2 6.8 copy-start.16
  7.2 7.7 copy-start.39
  7.2 77.1 %all-gather.6.cloned.1.call-start = ((), (), s32[]{:S(2)}) async-start(), calls=%async_computation.5 | async-start | bytes 7962624 | tf_op jit(solution)/shard_map/all_gather | solution.py:143
  9.8 21.7 %copy-start.49 = (s32[2,640]{1,0:T(2,128)S(1)}, s32[2,640]{1,0:T(2,128)}, u32[]{:S(2)}) copy-start(s32[2,640]{1,0:T(2,128)} %param.26) | copy-start | bytes 15364
  9.8 22.4 %copy-start.4 = (bf16[2,640,768]{2,1,0:T(8,128)(2,1)S(1)}, bf16[2,640,768]{2,1,0:T(8,128)(2,1)}, u32[]{:S(2)}) copy-start(bf16[2,640,768]{2,1,0:T(8,128)(2,1)} %param.24) | copy-start | bytes 5898244
  9.8 244.5 %all-gather.8.cloned.1.call-start = ((), (), s32[]{:S(2)}) async-start(), calls=%async_computation.6 | async-start | bytes 1327104 | tf_op jit(solution)/shard_map/all_gather | solution.py:144
  11.7 249.8 %all-gather.10.cloned.1.call-start = ((), (), s32[]{:S(2)}) async-start(), calls=%async_computation.7 | async-start | bytes 5308416 | tf_op jit(solution)/shard_map/all_gather | solution.py:145
  13.9 293.7 %all-gather.12.cloned.1.call-start = ((), (), s32[]{:S(2)}) async-start(), calls=%async_computation.8 | async-start | bytes 5308416 | tf_op jit(solution)/shard_map/all_gather | solution.py:146
  14.9 719.6 %reduce-scatter.10.cloned.1.call-start = ((), (), s32[]{:S(2)}) async-start(), calls=%async_computation.9 | async-start | bytes 2654208 | tf_op jit(solution)/shard_map/reduce_scatter | solution.py:276
  31.5 70.1 %copy-start.36 = (f32[768]{0:T(1024)}, f32[768]{0:T(1024)S(1)}, u32[]{:S(2)}) copy-start(f32[768]{0:T(1024)S(1)} %get-tuple-element.339) | copy-start | bytes 9220
  31.6 80.2 %copy-start.34 = (pred[1280]{0:T(1024)(128)(4,1)}, pred[1280]{0:T(1024)(128)(4,1)S(1)}, u32[]{:S(2)}) copy-start(pred[1280]{0:T(1024)(128)(4,1)S(1)} %broadcast_in_dim.127) | copy-start | bytes 3844
  138.6 8.2 copy-start.10
  149.0 6.7 copy-start.32
  156.2 11.2 %copy-start.2 = (bf16[2,640,12,64]{1,3,2,0:T(8,128)(2,1)S(1)}, bf16[2,640,12,64]{1,3,2,0:T(8,128)(2,1)}, u32[]{:S(2)}) copy-start(bf16[2,640,12,64]{1,3,2,0:T(8,128)(2,1)} %get-tuple-element.653) | copy-start | bytes 5898244 | tf_op jit(solution)/shard_map/while
  202.7 11.2 %copy-start.2 = (bf16[2,640,12,64]{1,3,2,0:T(8,128)(2,1)S(1)}, bf16[2,640,12,64]{1,3,2,0:T(8,128)(2,1)}, u32[]{:S(2)}) copy-start(bf16[2,640,12,64]{1,3,2,0:T(8,128)(2,1)} %get-tuple-element.653) | copy-start | bytes 5898244 | tf_op jit(solution)/shard_map/while
  248.3 6.0 copy-start
  248.4 6.0 copy-start.25
  248.4 6.0 copy-start.27
  248.4 6.0 copy-start.52
  258.9 1.9 copy-start.7
  258.9 2.6 copy-start.41
  258.9 2.5 copy-start.48
  258.9 2.5 copy-start.50
  261.5 46.2 %copy-start.51 = (f32[768]{0:T(1024)S(1)}, f32[768]{0:T(1024)}, u32[]{:S(2)}) copy-start(f32[768]{0:T(1024)} %get-tuple-element.341) | copy-start | bytes 9220
  318.8 1.5 copy-start.5
  319.4 3.7 copy-start.38
  319.4 3.7 copy-start.43
  351.0 13.4 %copy-start.8 = (f32[1280,768]{1,0:T(8,128)S(1)}, f32[1280,768]{1,0:T(8,128)}, u32[]{:S(2)}) copy-start(f32[1280,768]{1,0:T(8,128)} %copy-done.7) | copy-start | bytes 11796484
  364.5 4.0 copy-start.20
  366.5 1.9 copy-start.18
  371.6 364.5 %reduce-scatter.12.cloned.1.call-start = ((), (), s32[]{:S(2)}) async-start(), calls=%async_computation.10 | async-start | bytes 10616832 | tf_op jit(solution)/shard_map/reduce_scatter | solution.py:277
  384.5 353.7 %reduce-scatter.14.cloned.1.call-start = ((), (), s32[]{:S(2)}) async-start(), calls=%async_computation.11 | async-start | bytes 10616832 | tf_op jit(solution)/shard_map/reduce_scatter | solution.py:278
  396.7 471.6 %reduce-scatter.16.cloned.1.call-start = ((), (), s32[]{:S(2)}) async-start(), calls=%async_computation.12 | async-start | bytes 15925248
  404.1 8.2 copy-start.1
  404.1 8.2 copy-start.26
  404.1 8.2 copy-start.28
  404.1 8.2 copy-start.33
  412.8 11.5 %copy-start.3 = (bf16[2,640,12,64]{1,3,2,0:T(8,128)(2,1)S(1)}, bf16[2,640,12,64]{1,3,2,0:T(8,128)(2,1)}, u32[]{:S(2)}) copy-start(bf16[2,640,12,64]{1,3,2,0:T(8,128)(2,1)} %get-tuple-element.689) | copy-start | bytes 5898244 | tf_op jit(solution)/shard_map/while
  533.8 11.2 %copy-start.3 = (bf16[2,640,12,64]{1,3,2,0:T(8,128)(2,1)S(1)}, bf16[2,640,12,64]{1,3,2,0:T(8,128)(2,1)}, u32[]{:S(2)}) copy-start(bf16[2,640,12,64]{1,3,2,0:T(8,128)(2,1)} %get-tuple-element.689) | copy-start | bytes 5898244 | tf_op jit(solution)/shard_map/while
  684.1 5.9 copy-start.35
  692.4 1.8 copy-start.13
  693.5 5.1 copy-start.55
  694.4 4.3 copy-start.29
  725.9 1.6 copy-start.11
  725.9 7.3 copy-start.42
  726.0 7.3 copy-start.54
  726.0 7.3 copy-start.53
  726.0 7.3 copy-start.47
  726.0 7.3 copy-start.45
  726.0 7.3 copy-start.46
  726.0 174.2 %reduce-scatter.18.cloned.1.call-start = ((), (), s32[]{:S(2)}) async-start(), calls=%async_computation.13 | async-start | bytes 442368
  734.4 245.5 %all-reduce.3.cloned.1.call-start = ((), (), s32[]{:S(2)}) async-start(), calls=%async_computation.14 | async-start | bytes 5013504 | tf_op jit(solution)/shard_map/psum | solution.py:285
  991.2 33.7 %copy-start.14 = (bf16[96,4608]{0,1:T(8,128)(2,1)S(1)}, bf16[96,4608]{0,1:T(8,128)(2,1)}, u32[]{:S(2)}) copy-start(bf16[96,4608]{0,1:T(8,128)(2,1)} %get-tuple-element.392) | copy-start | bytes 2654212
  1031.9 6.1 copy-start.9
  1034.9 4.8 copy-start.15
  1037.9 3.2 copy-start.40
  1042.4 4.9 copy-start.17
  1042.4 4.9 copy-start.19
  1042.4 4.9 copy-start.22
  1042.4 4.9 copy-start.23
  1047.4 2.7 copy-start.21
  1047.4 2.6 copy-start.24
  1047.4 2.6 copy-start.30
  1047.4 2.6 copy-start.31
  (5 other events, 6.6 us)
Sparse Core Ops, SparseCore 0:
  10.3 74.0 all-gather.5
  86.6 21.3 all-gather.7
  110.1 51.4 all-gather.9
  163.7 50.5 all-gather.11
  371.7 34.8 reduce-scatter.9
  408.7 98.5 reduce-scatter.11
  509.7 97.8 reduce-scatter.13
  726.1 142.2 reduce-scatter.15
  871.2 29.0 reduce-scatter.17
  904.6 75.2 all-reduce.2
where the time goes:
time: 1060 us
  matrix products  490 us (46%)
  waiting for transfers between devices  268 us (25%)
  local copies, waits for them, and re-layouts  149 us (14%)
  other arithmetic  88.2 us (8%)
  blocking collectives  42.5 us (4%)
  between operations  20.4 us (2%)
    unnamed x12, waiting for transfers between devices  150 us
    psum x1, waiting for transfers between devices, body(): lax.psum(shards[0].astype(jnp.bfloat16), 'wide').astype(jnp.float32)  68.4 us
    unnamed x127, local copies, waits for them, and re-layouts  59.1 us
    dot_general x4, matrix products, score_block(): jnp.einsum('ihd,jhd->hij', to_ents, keys_all, preferred_element_type=jnp....  57.5 us
    all_gather x1, waiting for transfers between devices, body(): lax.all_gather(projection.astype(jnp.bfloat16), 'narrow', axis=0, tiled=T...  50.2 us
    dot_general x1, matrix products, body(): jnp.dot(normed_half, expand_w, preferred_element_type=jnp.float32)  46.1 us
    dot_general x4, matrix products, score_block(): jnp.einsum('ihd,jhd->hij', to_words, keys_all, preferred_element_type=jnp...  43.6 us
    dot_general x2, matrix products, attend_back(): jnp.einsum('hij,ihd->jhd', grad_sw, to_words, preferred_element_type=jnp....  43.2 us
  transfers between devices with their start and end apart: 10, of which 4 were waited for; matrix products, arithmetic and copies ran while one was open for 57% of the time, Pallas kernels for 0%

commit v1 on v0

v1 whole, which is shorter than its diff:
```python
import functools

import jax
import jax.numpy as jnp
from jax import lax
from jax.experimental import pallas as pl
from jax.experimental.pallas import tpu as pltpu
from jax.sharding import PartitionSpec as P

HEAD = 64
STEP = 10
LANES = 128
GROUP = 6 * HEAD
LOG2E = 1.4426950408889634
FAR = -1e30
VMEM_LIMIT = 60 * 1024 * 1024

beta_one = 0.9
beta_two = 0.999
adam_eps = 1e-08
norm_eps = 1e-05
clip_limit = 1.0
rate_table = (0.03, 0.3, 0.03, 0.015, 0.4)
decay_table = (0.01, 0.01, 0.01, 0.01, 0.0)

F32 = jnp.float32
BF16 = jnp.bfloat16


def mm(a, b):
    return lax.dot_general(a, b, (((1,), (0,)), ((), ())), preferred_element_type=F32)


def mm_nt(a, b):
    return lax.dot_general(a, b, (((1,), (1,)), ((), ())), preferred_element_type=F32)


def mm_tn(a, b):
    return lax.dot_general(a, b, (((0,), (0,)), ((), ())), preferred_element_type=F32)


def low_lanes(rows):
    return lax.broadcasted_iota(jnp.int32, (rows, LANES), 1) < HEAD


def swap_halves(tile):
    return pltpu.roll(tile, HEAD, 1)


def split_three(col):
    high = col.astype(BF16).astype(F32)
    rest = col - high
    mid = rest.astype(BF16).astype(F32)
    return high, mid, rest - mid


def qkv_tile(prod, bias, word):
    full = prod + bias
    query = jnp.where(word, full[:, 0:LANES], full[:, LANES : 2 * LANES])
    return (query.astype(BF16).astype(F32) * (HEAD**-0.5)).astype(BF16), full[
        :, 2 * LANES :
    ].astype(BF16)


def qkv_kernel(x_ref, w_ref, b_ref, word_ref, q_ref, kv_ref):
    word = word_ref[...] > 0
    for part in range(2):
        cols = slice(part * GROUP, (part + 1) * GROUP)
        query, keyval = qkv_tile(mm(x_ref[...], w_ref[:, cols]), b_ref[:, cols], word)
        out = slice(part * LANES, (part + 1) * LANES)
        q_ref[:, out] = query
        kv_ref[:, out] = keyval


def qkv_call(x, w, bias, word):
    rows, width = x.shape
    steps = w.shape[1] // (2 * GROUP)
    out = jax.ShapeDtypeStruct((rows, steps * 2 * LANES), BF16)
    return pl.pallas_call(
        qkv_kernel,
        grid=(steps,),
        in_specs=[
            pl.BlockSpec((rows, width), lambda i: (0, 0)),
            pl.BlockSpec((width, 2 * GROUP), lambda i: (0, i)),
            pl.BlockSpec((1, 2 * GROUP), lambda i: (0, i)),
            pl.BlockSpec((rows, LANES), lambda i: (0, 0)),
        ],
        out_specs=[pl.BlockSpec((rows, 2 * LANES), lambda i: (0, i))] * 2,
        out_shape=[out, out],
        compiler_params=pltpu.CompilerParams(vmem_limit_bytes=VMEM_LIMIT),
        name="qkv",
    )(x, w, bias, word)


def key_pair(keyval, kmask, low):
    wide = keyval.astype(F32)
    return (jnp.where(low, wide, swap_halves(wide)) * kmask.astype(F32)).astype(BF16)


def attend_kernel(q_ref, kv_ref, qa_ref, ka_ref, km_ref, ctx_ref, aug_ref):
    rows = q_ref.shape[0]
    low = low_lanes(rows)
    lane = lax.broadcasted_iota(jnp.int32, (rows, LANES), 1)
    outs = []
    for part in range(2):
        cols = slice(part * LANES, (part + 1) * LANES)
        keyval = kv_ref[:, cols]
        keys = jnp.concatenate([key_pair(keyval, km_ref[...], low), ka_ref[...]], axis=1)
        query = jnp.concatenate([q_ref[:, cols], qa_ref[...]], axis=1)
        scores = mm_nt(query, keys)
        top = jnp.max(scores, axis=1, keepdims=True)
        weight = jnp.exp2((scores - top) * LOG2E).astype(BF16)
        ones_val = jnp.where(low, 1.0, keyval.astype(F32)).astype(BF16)
        both = mm(weight, ones_val)
        total = swap_halves(both)
        outs.append(both / total)
        log_total = top + jnp.log(jnp.where(low, both, total))
        high, mid, rest = split_three(log_total)
        extra = jnp.where(lane == 8, -high, jnp.where(lane == 9, -mid, jnp.where(lane == 10, -rest, 0.0)))
        aug_ref[:, cols] = jnp.where(lane < 8, qa_ref[...].astype(F32), extra).astype(BF16)
    ctx_ref[...] = jnp.where(low, swap_halves(outs[0]), outs[1]).astype(BF16)


def attend_call(q, kv, qa, ka, km, length):
    rows, cols = q.shape
    seqs, steps = rows // length, cols // (2 * LANES)
    pair = pl.BlockSpec((length, 2 * LANES), lambda s, i: (s, i))
    one = pl.BlockSpec((length, LANES), lambda s, i: (s, 0))
    return pl.pallas_call(
        attend_kernel,
        grid=(seqs, steps),
        in_specs=[pair, pair, one, one, one],
        out_specs=[pl.BlockSpec((length, LANES), lambda s, i: (s, i)), pair],
        out_shape=[
            jax.ShapeDtypeStruct((rows, cols // 2), BF16),
            jax.ShapeDtypeStruct((rows, cols), BF16),
        ],
        compiler_params=pltpu.CompilerParams(vmem_limit_bytes=VMEM_LIMIT),
        name="attend",
    )(q, kv, qa, ka, km)


def attend_back_head(query, keyval, aug, gcon, con, kaug, kmask, word, odd, low, lane):
    keys = key_pair(keyval, kmask, low)
    scores_t = mm_nt(jnp.concatenate([keys, kaug], axis=1), jnp.concatenate([query, aug], axis=1))
    probs_t = jnp.exp2(scores_t * LOG2E)
    gwide = gcon.astype(F32)
    prod = gwide * con.astype(F32)
    mine = low != odd
    delta = jnp.sum(jnp.where(mine, prod, 0.0), axis=1, keepdims=True)
    high, mid, rest = split_three(delta)
    extra = jnp.where(lane == 0, -high, jnp.where(lane == 1, -mid, jnp.where(lane == 2, -rest, 0.0)))
    ghead = jnp.where(low, extra, jnp.where(odd, gwide, swap_halves(gwide))).astype(BF16)
    ones_val = jnp.where(low, jnp.where(lane < 3, 1.0, 0.0), keyval.astype(F32)).astype(BF16)
    gscores_t = (probs_t * mm_nt(ones_val, ghead)).astype(BF16)
    gval = mm(probs_t.astype(BF16), ghead)
    gkey = mm(gscores_t, query)
    gquery = (jnp.transpose(mm_tn(keys, gscores_t)) * (HEAD**-0.5)).astype(BF16)
    zero = jnp.zeros_like(gquery)
    gkey = jnp.where(kmask.astype(F32) > 0, gkey, 0.0)
    gkey = gkey + swap_halves(gkey)
    return (
        jnp.where(word, gquery, zero),
        jnp.where(word, zero, gquery),
        jnp.where(low, gkey, gval).astype(BF16),
    )


def attend_back_kernel(
    length, x_ref, q_ref, kv_ref, aug_ref, gc_ref, ctx_ref, ka_ref, km_ref, word_ref, gp_ref, gw_ref, sum_ref, xt
):
    step = pl.program_id(0)
    rows = x_ref.shape[0]

    @pl.when(step == 0)
    def _():
        xt[...] = jnp.transpose(x_ref[...])

    low = low_lanes(length)
    lane = lax.broadcasted_iota(jnp.int32, (length, LANES), 1)
    odd = lax.rem(step, 2) == 1
    for seq in range(rows // length):
        here = slice(seq * length, (seq + 1) * length)
        tiles = attend_back_head(
            q_ref[here], kv_ref[here], aug_ref[here], gc_ref[here], ctx_ref[here],
            ka_ref[here], km_ref[here], word_ref[here] > 0, odd, low, lane,
        )
        for index, tile in enumerate(tiles):
            gp_ref[here, index * LANES : (index + 1) * LANES] = tile
    grads = gp_ref[...]
    gw_ref[...] = mm(xt[...], grads).astype(BF16)
    sums = jnp.sum(grads.astype(F32).reshape(rows // 8, 8, GROUP), axis=0)
    sum_ref[...] = jnp.sum(sums, axis=0, keepdims=True)


def attend_back_call(x, q, kv, aug, gc, ctx, ka, km, word, length):
    rows, width = x.shape
    heads = q.shape[1] // LANES
    head = pl.BlockSpec((rows, LANES), lambda h: (0, h))
    pair = pl.BlockSpec((rows, LANES), lambda h: (0, h // 2))
    one = pl.BlockSpec((rows, LANES), lambda h: (0, 0))
    return pl.pallas_call(
        functools.partial(attend_back_kernel, length),
        grid=(heads,),
        in_specs=[pl.BlockSpec((rows, width), lambda h: (0, 0)), head, head, head, pair, pair, one, one, one],
        out_specs=[
            pl.BlockSpec((rows, GROUP), lambda h: (0, h)),
            pl.BlockSpec((width, GROUP), lambda h: (0, h)),
            pl.BlockSpec((1, GROUP), lambda h: (0, h)),
        ],
        out_shape=[
            jax.ShapeDtypeStruct((rows, heads * GROUP), BF16),
            jax.ShapeDtypeStruct((width, heads * GROUP), BF16),
            jax.ShapeDtypeStruct((1, heads * GROUP), F32),
        ],
        scratch_shapes=[pltpu.VMEM((width, rows), BF16)],
        compiler_params=pltpu.CompilerParams(vmem_limit_bytes=VMEM_LIMIT),
        name="attend_back",
    )(x, q, kv, aug, gc, ctx, ka, km, word)


def gelu_pair(pre):
    size = jnp.abs(pre) * (0.5**0.5)
    bell = jnp.exp2(pre * pre * (-0.5 * LOG2E))
    t = 1.0 / (1.0 + 0.3275911 * size)
    poly = t * (0.254829592 + t * (-0.284496736 + t * (1.421413741 + t * (-1.453152027 + t * 1.061405429))))
    tail = 0.5 * poly * bell
    share = jnp.where(pre >= 0, 1.0 - tail, tail)
    return pre * share, share + pre * bell * 0.3989422804014327


def fold(array_in):
    rows, cols = array_in.shape
    return jnp.sum(array_in.reshape(rows // 8, 8, cols), axis=0)


def middle_kernel(
    tiles, x_ref, ctx_ref, cot_ref, vec_ref, wo_hbm, w1_hbm, w2_hbm,
    out_ref, gr1_ref, gctx_ref, gw2_ref, gw1_ref, gwo_ref, gvec_ref,
    wo, w1, w2, h1_s, act_s, gb_s, gp_s, ga_s, ctx_s, dg_s, acc, sems,
):
    step = pl.program_id(0)
    size, width = x_ref.shape
    inner = w1.shape[1]
    chunks = inner // width

    def weight_copies():
        return (
            pltpu.make_async_copy(wo_hbm, wo, sems.at[0]),
            pltpu.make_async_copy(w1_hbm, w1, sems.at[1]),
            pltpu.make_async_copy(w2_hbm, w2, sems.at[2]),
        )

    @pl.when(step == 0)
    def _():
        for copy in weight_copies():
            copy.start()
        acc[...] = jnp.zeros_like(acc)

    def vec(row):
        return vec_ref[row : row + 1, :].astype(F32)

    @pl.when(step < tiles)
    def _():
        here = pl.ds(pl.multiple_of(step * size, size), size)

        @pl.when(step == 0)
        def _():
            weight_copies()[0].wait()

        ctx_s[here, :] = ctx_ref[...]
        resid = x_ref[...].astype(F32) + mm(ctx_ref[...], wo[...]) + vec(5)
        center = resid - jnp.mean(resid, axis=1, keepdims=True)
        inv1 = lax.rsqrt(jnp.mean(center * center, axis=1, keepdims=True) + norm_eps)
        n1 = center * inv1
        h1 = n1 * vec(6) + vec(7)
        h1b = h1.astype(BF16)
        h1_s[here, :] = h1b

        @pl.when(step == 0)
        def _():
            weight_copies()[1].wait()
            weight_copies()[2].wait()

        branch = h1 + vec(8)
        for c in range(chunks):
            cols = slice(c * width, (c + 1) * width)
            act, slope = gelu_pair(mm(h1b, w1[:, cols]) + vec(11 + c))
            act = act.astype(BF16)
            act_s[here, cols] = act
            dg_s[:, cols] = slope
            branch = branch + mm(act, w2[cols, :])
        center = branch - jnp.mean(branch, axis=1, keepdims=True)
        inv2 = lax.rsqrt(jnp.mean(center * center, axis=1, keepdims=True) + norm_eps)
        n2 = center * inv2
        out_ref[...] = (n2 * vec(9) + vec(10)).astype(BF16)
        grad = cot_ref[...].astype(F32)
        gn = grad * n2
        acc[9] += fold(gn)
        acc[10] += fold(grad)
        scaled = grad * vec(9)
        gr2 = inv2 * (
            scaled
            - jnp.mean(scaled, axis=1, keepdims=True)
            - n2 * jnp.mean(scaled * n2, axis=1, keepdims=True)
        )
        gb = gr2.astype(BF16)
        gb_s[here, :] = gb
        acc[8] += fold(gb.astype(F32))
        gh1 = gr2
        for c in range(chunks):
            cols = slice(c * width, (c + 1) * width)
            gpre = (mm_nt(gb, w2[cols, :]) * dg_s[:, cols]).astype(BF16)
            gp_s[here, cols] = gpre
            acc[11 + c] += fold(gpre.astype(F32))
            gh1 = gh1 + mm_nt(gpre, w1[:, cols])
        acc[6] += fold(gh1 * n1)
        acc[7] += fold(gh1)
        scaled = gh1 * vec(6)
        gr1 = inv1 * (
            scaled
            - jnp.mean(scaled, axis=1, keepdims=True)
            - n1 * jnp.mean(scaled * n1, axis=1, keepdims=True)
        )
        gr1_ref[...] = gr1
        ga = gr1.astype(BF16)
        ga_s[here, :] = ga
        acc[5] += fold(ga.astype(F32))
        gctx_ref[...] = mm_nt(ga, wo[...]).astype(BF16)

    for c in range(chunks):
        cols = slice(c * width, (c + 1) * width)

        @pl.when(step == tiles + c)
        def _():
            gw2_ref[...] = mm_tn(act_s[:, cols], gb_s[...]).astype(BF16)

        @pl.when(step == tiles + chunks + c)
        def _():
            gw1_ref[...] = mm_tn(h1_s[...], gp_s[:, cols]).astype(BF16)

    @pl.when(step == tiles + 2 * chunks)
    def _():
        gwo_ref[...] = mm_tn(ctx_s[...], ga_s[...]).astype(BF16)
        for row in range(acc.shape[0]):
            gvec_ref[row : row + 1, :] = jnp.sum(acc[row], axis=0, keepdims=True)


def middle_call(x, ctx, cot, vec, wo, w1, w2, size):
    rows, width = x.shape
    inner = w1.shape[1]
    tiles, chunks = rows // size, inner // width
    tile = pl.BlockSpec((size, width), lambda i: (jnp.minimum(i, tiles - 1), 0))
    hbm = pl.BlockSpec(memory_space=pl.ANY)

    def after(start):
        return lambda i: jnp.clip(i - start, 0, chunks - 1)

    shape = jax.ShapeDtypeStruct
    return pl.pallas_call(
        functools.partial(middle_kernel, tiles),
        grid=(tiles + 2 * chunks + 1,),
        in_specs=[tile, tile, tile, pl.BlockSpec(vec.shape, lambda i: (0, 0)), hbm, hbm, hbm],
        out_specs=[
            tile,
            tile,
            tile,
            pl.BlockSpec((width, width), lambda i: (after(tiles)(i), 0)),
            pl.BlockSpec((width, width), lambda i: (0, after(tiles + chunks)(i))),
            pl.BlockSpec((width, width), lambda i: (0, 0)),
            pl.BlockSpec(vec.shape, lambda i: (0, 0)),
        ],
        out_shape=[
            shape((rows, width), BF16),
            shape((rows, width), F32),
            shape((rows, width), BF16),
            shape((inner, width), BF16),
            shape((width, inner), BF16),
            shape((width, width), BF16),
            shape(vec.shape, F32),
        ],
        scratch_shapes=[
            pltpu.VMEM((width, width), BF16),
            pltpu.VMEM((width, inner), BF16),
            pltpu.VMEM((inner, width), BF16),
            pltpu.VMEM((rows, width), BF16),
            pltpu.VMEM((rows, inner), BF16),
            pltpu.VMEM((rows, width), BF16),
            pltpu.VMEM((rows, inner), BF16),
            pltpu.VMEM((rows, width), BF16),
            pltpu.VMEM((rows, width), BF16),
            pltpu.VMEM((size, inner), F32),
            pltpu.VMEM((vec.shape[0], 8, width), F32),
            pltpu.SemaphoreType.DMA((3,)),
        ],
        compiler_params=pltpu.CompilerParams(vmem_limit_bytes=VMEM_LIMIT),
        name="middle",
    )(x, ctx, cot, vec, wo, w1, w2)


def input_grad_kernel(gp_ref, w_ref, gr1_ref, out_ref):
    out_ref[...] = (gr1_ref[...] + mm_nt(gp_ref[...], w_ref[...])).astype(BF16)


def input_grad_call(gp, w, gr1, size):
    rows, cols = gp.shape
    width = w.shape[0]
    return pl.pallas_call(
        input_grad_kernel,
        grid=(rows // size,),
        in_specs=[
            pl.BlockSpec((size, cols), lambda i: (i, 0)),
            pl.BlockSpec((width, cols), lambda i: (0, 0)),
            pl.BlockSpec((size, width), lambda i: (i, 0)),
        ],
        out_specs=pl.BlockSpec((size, width), lambda i: (i, 0)),
        out_shape=jax.ShapeDtypeStruct((rows, width), BF16),
        compiler_params=pltpu.CompilerParams(vmem_limit_bytes=VMEM_LIMIT),
        name="input_grad",
    )(gp, w, gr1)


def adam_update(master, first_old, second_old, grad_shard, factor, index):
    clipped = grad_shard * factor
    new_first = beta_one * first_old + (1.0 - beta_one) * clipped
    new_second = beta_two * second_old + (1.0 - beta_two) * clipped * clipped
    direction = (
        new_first
        / (1.0 - beta_one**STEP)
        / (jnp.sqrt(new_second / (1.0 - beta_two**STEP)) + adam_eps)
    )
    new_weight = master - rate_table[index] * (direction + decay_table[index] * master)
    return (new_weight, new_first, new_second)


def by_head(array_in):
    rows, cols = array_in.shape
    heads = cols // GROUP
    return array_in.reshape(rows, 6, heads, HEAD).transpose(0, 2, 1, 3).reshape(rows, cols)


def by_block(array_in):
    rows, cols = array_in.shape
    heads = cols // GROUP
    return array_in.reshape(rows, heads, 6, HEAD).transpose(0, 2, 1, 3).reshape(rows, cols)


def body(
    x_in, cotangent, segment_ids, type_ids,
    projection, context_out, expand_weight, reduce_weight, vector_params,
    first_projection, first_context, first_expand, first_reduce, first_vectors,
    second_projection, second_context, second_expand, second_reduce, second_vectors,
):
    seq_count, seq_len, width = x_in.shape
    rows = seq_count * seq_len

    def gather(array_in, axis):
        return lax.all_gather(array_in.astype(BF16), "narrow", axis=axis, tiled=True)

    proj_w = gather(by_head(projection), 0)
    vec_half = gather(vector_params, 1)
    ctx_w, expand_w, reduce_w = gather(context_out, 0), gather(expand_weight, 0), gather(reduce_weight, 0)

    hidden = x_in.reshape(rows, width)
    cot = cotangent.reshape(rows, width)
    word_col = (type_ids == 0).reshape(rows, 1)
    lane = lax.broadcasted_iota(jnp.int32, (rows, LANES), 1)
    word = jnp.broadcast_to(word_col, (rows, LANES)).astype(BF16)
    kmask = ((lane < HEAD) == word_col).astype(BF16)
    same = segment_ids.reshape(rows, 1) == lane
    qaug = jnp.where(same & (lane < 8), 1.0, 0.0).astype(BF16)
    kaug = jnp.where(lane < 8, jnp.where(same, 0.0, FAR), jnp.where(lane < 11, 1.0, 0.0)).astype(BF16)

    zero_row = jnp.zeros((1, width), BF16)
    bias = by_head(jnp.concatenate([vec_half[0:4], zero_row, vec_half[4:5]]).reshape(1, -1)).astype(F32)

    query, keyval = qkv_call(hidden, proj_w, bias, word)
    context, aug = attend_call(query, keyval, qaug, kaug, kmask, seq_len)
    block_out, grad_r1, grad_context, grad_reduce, grad_expand, grad_ctx_w, grad_mid = middle_call(
        hidden, context, cot, vec_half, ctx_w, expand_w, reduce_w, 256
    )
    grad_proj, grad_proj_w, grad_sums = attend_back_call(
        hidden, query, keyval, aug, grad_context, context, kaug, kmask, word, seq_len
    )
    input_grad = input_grad_call(grad_proj, proj_w, grad_r1, 256)
    sum_rows = by_block(grad_sums).reshape(6, width)
    grad_vectors = jnp.concatenate([sum_rows[0:4], sum_rows[5:6], grad_mid[5:]], axis=0)

    def scatter(array_in, axis):
        return lax.psum_scatter(array_in, "narrow", scatter_dimension=axis, tiled=True)

    def over_wide(array_in):
        return lax.psum(array_in.astype(BF16), "wide").astype(F32)

    shards = (
        by_block(over_wide(scatter(grad_proj_w, 0))),
        over_wide(scatter(grad_ctx_w, 0)),
        over_wide(scatter(grad_expand, 0)),
        over_wide(scatter(grad_reduce, 0)),
        over_wide(scatter(grad_vectors, 1)),
    )
    masters = (projection, context_out, expand_weight, reduce_weight, vector_params)
    firsts = (first_projection, first_context, first_expand, first_reduce, first_vectors)
    seconds = (second_projection, second_context, second_expand, second_reduce, second_vectors)
    local_squares = sum((jnp.sum(shard_item * shard_item) for shard_item in shards))
    total_squares = lax.psum(local_squares, "narrow")
    grad_norm = jnp.sqrt(total_squares)
    factor = jnp.minimum(1.0, clip_limit / (grad_norm + 1e-06))
    results = [
        adam_update(masters[index], firsts[index], seconds[index], shards[index], factor, index)
        for index in range(5)
    ]
    out_shape = (seq_count, seq_len, width)
    return (
        block_out.reshape(out_shape),
        input_grad.reshape(out_shape),
        grad_norm,
        *(item[0] for item in results),
        *(item[1] for item in results),
        *(item[2] for item in results),
        *(item[0].astype(BF16) for item in results),
    )


def solution(mesh):
    shard, col = P("narrow", None), P(None, "narrow")
    seqs = P(("wide", "narrow"), None, None)
    group = (shard, shard, shard, shard, col)
    return jax.shard_map(
        body,
        mesh=mesh,
        in_specs=(seqs, seqs, P(("wide", "narrow"), None), P(("wide", "narrow"), None), *group, *group, *group),
        out_specs=(seqs, seqs, P(), *group, *group, *group, *group),
        check_vma=False,
    )
```

time: 1060 us -> 710 us (0.67)
  matrix products: 490 us -> 0 us
  Pallas kernels: 0 us -> 188 us
  waiting for transfers between devices: 268 us -> 392 us
  local copies, waits for them, and re-layouts: 149 us -> 30 us
  other arithmetic: 88.2 us -> 29.3 us
    dot_general x32 -> x0, matrix products: 490 us -> none  [the longest x4 57.5 us: score_block(): jnp.einsum('ihd,jhd->hij', to_ents, keys_all, preferred_element_type=jnp....]
    pallas_call x0 -> x5, Pallas kernels: none -> 188 us  [the longest x1 80.5 us: middle_call(): pl.pallas_call(functools.partial(middle_kernel, tiles), grid=(tiles + 2 *...]
    reduce_scatter x3 -> x4, waiting for transfers between devices: 0.02 us -> 168 us  [scatter(): lax.psum_scatter(array_in, 'narrow', scatter_dimension=axis, tiled=True)]
    unnamed x12 -> x11, waiting for transfers between devices: 150 us -> 27.2 us
    all_gather x4, waiting for transfers between devices: 50.2 us -> 134 us  [gather(): lax.all_gather(array_in.astype(BF16), 'narrow', axis=axis, tiled=True)]
    reshape x10 -> x1, local copies, waits for them, and re-layouts: 38.6 us -> 0.08 us  [by_block(): array_in.reshape(rows, heads, 6, HEAD).transpose(0, 2, 1, 3)]
    unnamed x127 -> x54, local copies, waits for them, and re-layouts: 59.1 us -> 20.8 us
    reduce_sum x10 -> x0, other arithmetic: 35.4 us -> none  [the longest x2 18.6 us: attend(): row_total = jnp.sum(exp_scores, axis=-1, keepdims=True)]
  transfers between devices with their start and end apart: 10 -> 10, of which waited for: 4 -> 8; matrix products, arithmetic and copies ran while one was open for 57% -> 3% of each run, Pallas kernels for 0% -> 13%
where the time goes in v1:
time: 710 us; the launch traced here: 702 us
  waiting for transfers between devices  392 us (55%)
  Pallas kernels  188 us (26%)
  blocking collectives  42.7 us (6%)
  local copies, waits for them, and re-layouts  30 us (4%)
  other arithmetic  29.3 us (4%)
  between operations  19.8 us (3%)
    reduce_scatter x4, waiting for transfers between devices, scatter(): lax.psum_scatter(array_in, 'narrow', scatter_dimension=axis, tiled=True)  168 us
    all_gather x4, waiting for transfers between devices, gather(): lax.all_gather(array_in.astype(BF16), 'narrow', axis=axis, tiled=True)  134 us
    pallas_call x1, Pallas kernels, middle_call(): pl.pallas_call(functools.partial(middle_kernel, tiles), grid=(tiles + 2 *...  80.5 us
    psum x1, waiting for transfers between devices, over_wide(): return lax.psum(array_in.astype(BF16), 'wide').astype(F32)  62.6 us
    pallas_call x1, Pallas kernels, attend_back_call(): pl.pallas_call(functools.partial(attend_back_kernel, length), grid=(heads...  48.8 us
    unnamed x11, waiting for transfers between devices  27.2 us
    pallas_call x1, Pallas kernels, attend_call(): pl.pallas_call(attend_kernel, grid=(seqs, steps), in_specs=[pair, pair, o...  26.4 us
    unnamed x54, local copies, waits for them, and re-layouts  20.8 us
  transfers between devices with their start and end apart: 10, of which 8 were waited for; matrix products, arithmetic and copies ran while one was open for 3% of the time, Pallas kernels for 13%

profile of v1, /device:TPU:0, one launch (start us, length us, event | category | flops | bytes accessed | tf_op | source)
XLA Modules:
  0.0 702.1 jit_solution(10214396840466110047)
XLA Ops:
  7.2 1.9 copy.63
  9.2 0.1 convert_element_type.78
  9.3 0.1 copy.64
  9.4 1.3 copy.65
  10.8 1.6 convert_element_type.91
  12.6 2.2 convert_element_type.92
  14.8 0.0 all-gather.12.cloned.1.call-start
  14.9 0.9 convert_element_type.93
  15.9 15.8 %all-gather = bf16[8,96,15]{1,2,0:T(8,128)(2,1)S(1)} all-gather(bf16[1,96,15]{1,2,0:T(8,128)(2,1)S(1)} %convert_bitcast_fusion), channel_id=1, replica_groups=mesh['wide'=4,'narrow'=8] {'narrow'}, dimensions={0}, use_global_device_ids=true | all-gather | bytes 25920 | tf_op jit(solution)/shard_map/all_gather | solution.py:458
  31.7 0.1 reshape.103
  31.8 0.7 broadcast_compare_fusion
  32.6 0.7 eq.24
  33.3 0.1 pad.4.clone
  33.3 0.1 maximum_convert_fusion
  33.4 0.1 reshape.101
  33.5 0.7 reshape.100.b_ref
  34.2 1.0 compare_convert_fusion.km_ref
  35.2 1.0 select_convert_fusion.1.qa_ref
  36.2 1.0 select_convert_fusion.ka_ref
  37.1 47.9 %all-gather.6.cloned.1.call-done.w_ref = bf16[768,4608]{1,0:T(8,128)(2,1)} async-done(((bf16[96,4608]{1,0:T(8,128)(2,1)}), bf16[768,4608]{1,0:T(8,128)(2,1)}) %all-gather.6.cloned.1.call-update) | async-done | bytes 7077904 | tf_op jit(solution)/shard_map/all_gather | solution.py:458
  85.0 1.0 broadcast_in_dim.32.word_ref
  85.9 16.7 %qkv.1 = (bf16[1280,1536]{1,0:T(8,128)(2,1)}, bf16[1280,1536]{1,0:T(8,128)(2,1)}) custom-call(bf16[1280,768]{1,0:T(8,128)(2,1)} %bitcast.30, bf16[768,4608]{1,0:T(8,128)(2,1)} %all-gather.6.cloned.1.call-done.w_ref, f32[1,4608]{1,0:T(1,128)} %reshape.100.b_ref, bf16[1280,128]{1,0:T(8,128)(2,1)} %broadcast_in_dim.32.word_ref), custom_call_target="tpu_custom_call" | custom-call | tf_op jit(solution)/shard_map/qkv/pallas_call | solution.py:79
  102.7 26.4 %attend.1 = (bf16[1280,768]{1,0:T(8,128)(2,1)}, bf16[1280,1536]{1,0:T(8,128)(2,1)}) custom-call(bf16[1280,1536]{1,0:T(8,128)(2,1)} %get-tuple-element.37.q_ref, bf16[1280,1536]{1,0:T(8,128)(2,1)} %get-tuple-element.38.kv_ref, bf16[1280,128]{1,0:T(8,128)(2,1)} %select_convert_fusion.1.qa_ref, bf16[1280,128]{1,0:T(8,128)(2,1)} %select_convert_fusion.ka_ref, ...), custom_call_target="tpu_custom_call" | custom-call | tf_op jit(solution)/shard_map/attend/pallas_call | solution.py:129
  129.1 33.2 %all-gather.10.cloned.1.call-done.w1_hbm = bf16[768,3072]{1,0:T(8,128)(2,1)} async-done(((bf16[96,3072]{1,0:T(8,128)(2,1)}), bf16[768,3072]{1,0:T(8,128)(2,1)}) %all-gather.10.cloned.1.call-update) | async-done | bytes 4718608 | tf_op jit(solution)/shard_map/all_gather | solution.py:458
  162.3 52.6 %all-gather.12.cloned.1.call-done.w2_hbm = bf16[3072,768]{1,0:T(8,128)(2,1)} async-done(((bf16[384,768]{1,0:T(8,128)(2,1)}), bf16[3072,768]{1,0:T(8,128)(2,1)}) %all-gather.12.cloned.1.call-update) | async-done | bytes 4718608 | tf_op jit(solution)/shard_map/all_gather | solution.py:458
  214.9 80.5 %middle.1 = (bf16[1280,768]{1,0:T(8,128)(2,1)}, f32[1280,768]{1,0:T(8,128)}, bf16[1280,768]{1,0:T(8,128)(2,1)}, bf16[3072,768]{1,0:T(8,128)(2,1)}, bf16[768,3072...) custom-call(bf16[1280,768]{1,0:T(8,128)(2,1)} %bitcast.31, ...), custom_call_target="tpu_custom_call" | custom-call | tf_op jit(solution)/shard_map/middle/pallas_call | solution.py:360
  295.5 0.5 reduce-scatter.12.cloned.1.call-update
  296.0 0.7 reduce-scatter.14.cloned.1.call-update
  296.8 48.8 %attend_back.1 = (bf16[1280,4608]{1,0:T(8,128)(2,1)}, bf16[768,4608]{1,0:T(8,128)(2,1)}, f32[1,4608]{1,0:T(1,128)}) custom-call(bf16[1280,768]{1,0:T(8,128)(2,1)} %bitcast.32, bf16[1280,1536]{1,0:T(8,128)(2,1)} %get-tuple-element.37.q_ref, bf16[1280,1536]{1,0:T(8,128)(2,1)} %get-tuple-element.38.kv_ref, bf16[1280,1536]{1,0:T(8,128)(2,1)} %get-tuple-element.41.aug_ref, ...), custom_call_target="tpu_custom_call" | custom-call | tf_op jit(solution)/shard_map/attend_back/pallas_call | solution.py:202
  345.7 0.7 copy-done.17
  346.5 0.1 reshape.99
  346.6 0.1 slice.26
  346.7 0.1 slice.24
  346.8 0.9 copy.79
  347.8 34.6 %reduce-scatter.12.cloned.1.call-done = bf16[96,3072]{1,0:T(8,128)(2,1)} async-done(((bf16[768,3072]{1,0:T(8,128)(2,1)}), bf16[96,3072]{1,0:T(8,128)(2,1)}) %reduce-scatter.12.cloned.1.call-update) | async-done | bytes 589840 | tf_op jit(solution)/shard_map/reduce_scatter | solution.py:490
  382.5 55.6 %reduce-scatter.14.cloned.1.call-done = bf16[384,768]{1,0:T(8,128)(2,1)} async-done(((bf16[3072,768]{1,0:T(8,128)(2,1)}), bf16[384,768]{1,0:T(8,128)(2,1)}) %reduce-scatter.14.cloned.1.call-update) | async-done | bytes 589840 | tf_op jit(solution)/shard_map/reduce_scatter | solution.py:490
  438.1 77.9 %reduce-scatter.8.cloned.1.call-done = bf16[96,4608]{1,0:T(8,128)(2,1)} async-done(((bf16[768,4608]{1,0:T(8,128)(2,1)}), bf16[96,4608]{1,0:T(8,128)(2,1)}) %reduce-scatter.8.cloned.1.call-update) | async-done | bytes 884752 | tf_op jit(solution)/shard_map/reduce_scatter | solution.py:490
  516.1 3.0 copy.69
  519.0 3.0 copy.72
  522.0 25.9 %reduce-scatter.16.cloned.1.call-done = f32[96,15]{1,0:T(8,128)} async-done(((f32[768,15]{1,0:T(8,128)}), f32[96,15]{1,0:T(8,128)}) %reduce-scatter.16.cloned.1.call-update) | async-done | bytes 5776
  547.9 0.9 copy.80
  548.7 10.0 %psum.46 = bf16[15,96]{1,0:T(8,128)(2,1)S(1)} all-reduce(bf16[15,96]{1,0:T(8,128)(2,1)S(1)} %copy.80), channel_id=1, replica_groups=mesh['wide'=4,'narrow'=8] {'wide'}, use_global_device_ids=true, to_apply=%region_13.14 | all-reduce | flops 1440 | bytes 5760 | tf_op jit(solution)/shard_map/psum | solution.py:493
  558.8 0.6 fusion.18
  559.4 62.6 %all-reduce.3.cloned.1.call-done = (bf16[96,4608]{1,0:T(8,128)(2,1)}, bf16[96,768]{1,0:T(8,128)(2,1)}, bf16[96,3072]{1,0:T(8,128)(2,1)}, bf16[384,768]{1,0:T(8,128)(2,1)}) async-done(((bf16[96,4608]{1,0:T(8,128)(2,1)}, bf16[96,768]{1,0:T(8,128)(2,1)}, bf16[96,3072]{1,0:T(8,128)(2,1)}, bf16[384,768]{1,0:T(8,128)(2,1)}), (bf16[96,4608]{1,0:T(8,128)(2,1)}, bf16[96,768]{1,0:T(8,128)(2,1)}, ...) | async-done | bytes 2211856 | tf_op jit(solution)/shard_map/psum | solution.py:493
  622.0 2.1 fusion.8
  624.1 2.0 fusion.7
  626.1 0.7 fusion.14
  626.8 1.1 fusion.2
  631.0 15.6 %input_grad.1 = bf16[1280,768]{1,0:T(8,128)(2,1)} custom-call(bf16[1280,4608]{1,0:T(8,128)(2,1)} %get-tuple-element.43.gp_ref, bf16[768,4608]{1,0:T(8,128)(2,1)} %all-gather.6.cloned.1.call-done.w_ref, f32[1280,768]{1,0:T(8,128)} %get-tuple-element.44.gr1_ref), custom_call_target="tpu_custom_call" | custom-call | tf_op jit(solution)/shard_map/input_grad/pallas_call | solution.py:408
  646.7 16.8 %psum.47 = f32[]{:T(128)} all-reduce(f32[]{:T(128)S(6)} %add.115), channel_id=1, replica_groups=mesh['wide'=4,'narrow'=8] {'narrow'}, use_global_device_ids=true, to_apply=%region_15.16 | all-reduce | flops 1 | bytes 8 | tf_op jit(solution)/shard_map/psum | solution.py:506
  664.3 1.4 convert_multiply_fusion
  665.6 3.0 copy.70
  668.6 2.0 copy.71
  670.6 0.4 copy-done
  671.0 0.7 copy-done.1
  671.7 4.2 fusion.32
  675.9 1.3 copy.78
  677.2 2.9 copy.75
  680.1 3.1 copy.76
  683.3 1.8 copy.77
  685.1 0.6 fusion.20
  685.8 1.1 fusion.29
  686.9 4.4 fusion.23
  691.3 2.6 fusion.26
  (76 shorter events, 0.8 us)
Async XLA Ops:
  7.2 77.8 %all-gather.6.cloned.1.call-start = ((), (), s32[]{:S(2)}) async-start(), calls=%async_computation.5 | async-start | bytes 7962624 | tf_op jit(solution)/shard_map/all_gather | solution.py:458
  10.8 118.3 %all-gather.8.cloned.1.call-start = ((), (), s32[]{:S(2)}) async-start(), calls=%async_computation.6 | async-start | bytes 1327104 | tf_op jit(solution)/shard_map/all_gather | solution.py:458
  12.5 2.4 copy-start.3
  12.5 149.8 %all-gather.10.cloned.1.call-start = ((), (), s32[]{:S(2)}) async-start(), calls=%async_computation.7 | async-start | bytes 5308416 | tf_op jit(solution)/shard_map/all_gather | solution.py:458
  14.8 1.0 copy-start.18
  14.8 200.1 %all-gather.12.cloned.1.call-start = ((), (), s32[]{:S(2)}) async-start(), calls=%async_computation.8 | async-start | bytes 5308416 | tf_op jit(solution)/shard_map/all_gather | solution.py:458
  15.8 332.0 %reduce-scatter.10.cloned.1.call-start = ((), (), s32[]{:S(2)}) async-start(), calls=%async_computation.10 | async-start | bytes 1327104 | tf_op jit(solution)/shard_map/reduce_scatter | solution.py:490
  31.8 70.9 %copy-start.16 = (bf16[768,15]{0,1:T(8,128)(2,1)}, bf16[768,15]{0,1:T(8,128)(2,1)S(1)}, u32[]{:S(2)}) copy-start(bf16[768,15]{0,1:T(8,128)(2,1)S(1)} %reshape.103) | copy-start | bytes 69124
  295.4 87.1 %reduce-scatter.12.cloned.1.call-start = ((), (), s32[]{:S(2)}) async-start(), calls=%async_computation.11 | async-start | bytes 5308416 | tf_op jit(solution)/shard_map/reduce_scatter | solution.py:490
  296.0 142.1 %reduce-scatter.14.cloned.1.call-start = ((), (), s32[]{:S(2)}) async-start(), calls=%async_computation.12 | async-start | bytes 5308416 | tf_op jit(solution)/shard_map/reduce_scatter | solution.py:490
  296.7 219.3 %reduce-scatter.8.cloned.1.call-start = ((), (), s32[]{:S(2)}) async-start(), calls=%async_computation.9 | async-start | bytes 7962624 | tf_op jit(solution)/shard_map/reduce_scatter | solution.py:490
  345.6 0.8 copy-start.17
  345.6 0.8 copy-start.19
  345.7 202.2 %reduce-scatter.16.cloned.1.call-start = ((), (), s32[]{:S(2)}) async-start(), calls=%async_computation.13 | async-start | bytes 442368
  347.8 274.3 %all-reduce.3.cloned.1.call-start = ((), (), s32[]{:S(2)}) async-start(), calls=%async_computation.14 | async-start | bytes 4423680 | tf_op jit(solution)/shard_map/psum | solution.py:493
  622.0 4.0 copy-start.12
  622.0 4.7 copy-start.6
  668.6 2.4 copy-start
  668.6 3.1 copy-start.1
  680.1 3.1 copy-start.2
  683.2 1.9 copy-start.20
  683.2 1.9 copy-start.21
  683.2 2.5 copy-start.9
  683.2 2.5 copy-start.13
  683.2 2.5 copy-start.14
  683.2 2.5 copy-start.15
  685.1 1.8 copy-start.4
  685.1 1.8 copy-start.8
  686.9 4.4 copy-start.5
  686.9 4.4 copy-start.7
  686.9 4.4 copy-start.10
  686.9 4.4 copy-start.11
Sparse Core Ops, SparseCore 0:
  10.9 74.0 all-gather.5
  87.2 21.3 all-gather.7
  110.8 51.4 all-gather.9
  164.3 50.5 all-gather.11
  295.5 31.6 reduce-scatter.9
  329.4 52.9 reduce-scatter.11
  384.8 53.2 reduce-scatter.13
  440.4 75.5 reduce-scatter.7
  518.9 28.9 reduce-scatter.15
  551.6 70.3 all-reduce.2

commit v2 on v1

--- a/solution.py
+++ b/solution.py
@@ -90,6 +90,318 @@
         compiler_params=pltpu.CompilerParams(vmem_limit_bytes=VMEM_LIMIT),
         name="qkv",
     )(x, w, bias, word)
+
+
+class Links:
+    def __init__(self, send, recv):
+        self.send, self.recv = send, recv
+        self.count = 0
+        self.slots = {}
+        self.open = []
+
+    def slot(self, key):
+        if key not in self.slots:
+            self.slots[key] = len(self.slots)
+        return self.slots[key]
+
+    def copy(self, key, src, dst, device):
+        index = self.slot(key)
+        return pltpu.make_async_remote_copy(
+            src_ref=src,
+            dst_ref=dst,
+            send_sem=self.send.at[index],
+            recv_sem=self.recv.at[index],
+            device_id=device,
+            device_id_type=pl.DeviceIdType.MESH,
+        )
+
+    def start(self, key, src, dst, device):
+        copy = self.copy(key, src, dst, device)
+        copy.start()
+        self.open.append(copy)
+
+    def arrived(self, key, dst, device):
+        self.copy(key, dst, dst, device).wait_recv()
+
+    def finish(self):
+        for copy in self.open:
+            copy.wait_send()
+        self.open = []
+
+
+class Place:
+    def __init__(self, narrow):
+        self.wide, self.me = lax.axis_index("wide"), lax.axis_index("narrow")
+        self.core = lax.rem(self.me, 2)
+        self.z = self.me // 2
+        self.depth = narrow // 2
+        self.x_quarter = self.wide + 1 - 2 * lax.rem(self.wide, 2)
+        self.y_quarter = lax.rem(self.wide + 2, 4)
+        self.d_quarter = lax.rem(self.x_quarter + 2, 4)
+        self.sib = self.me + 1 - 2 * self.core
+        self.x_dev, self.y_dev = {"wide": self.x_quarter}, {"wide": self.y_quarter}
+        self.sib_dev = {"narrow": self.sib}
+
+    def ahead(self, k):
+        return 2 * lax.rem(self.z + k, self.depth) + self.core
+
+    def behind(self, k, other=False):
+        core = 1 - self.core if other else self.core
+        return 2 * lax.rem(self.z + self.depth - k, self.depth) + core
+
+    def z_dev(self, k):
+        return {"narrow": self.ahead(k)}
+
+    def greet(self):
+        barrier = pltpu.get_barrier_semaphore()
+        partners = [self.x_dev, self.y_dev, self.sib_dev] + [self.z_dev(k) for k in range(1, self.depth)]
+        for device in partners:
+            pl.semaphore_signal(barrier, inc=1, device_id=device, device_id_type=pl.DeviceIdType.MESH)
+        pl.semaphore_wait(barrier, len(partners))
+
+
+def spot(start, size, unit):
+    return pl.ds(pl.multiple_of(start, unit), size)
+
+
+def gather_kernel(
+    narrow, x_ref, proj_ref, wo_ref, w1_ref, w2_ref, vec_ref, word_ref,
+    q_out, kv_out, a_out, e_out, w2_out, vec_out,
+    a_full, e_own, w2_own, v_all, bias, q_s, kv_s, send, recv, local,
+):
+    rows, width = x_ref.shape
+    share = proj_ref.shape[0]
+    deep = w2_ref.shape[0]
+    half, quarter, equarter, dquarter = share // 2, proj_ref.shape[1] // 4, e_own.shape[1] // 4, deep // 4
+    heads = width // HEAD
+    here = Place(narrow)
+    links = Links(send, recv)
+    me, steps = here.me, range(1, here.depth)
+
+    def region(kind, owner, part, side=None):
+        size, start = (share, 0) if side is None else (half, side * half)
+        if kind == "a":
+            return a_full.at[spot(owner * share + start, size, 16), spot(part * quarter, quarter, LANES)]
+        if kind == "e":
+            return e_out.at[spot(owner * share + start, size, 16), spot(part * equarter, equarter, LANES)]
+        size, start = (dquarter, 0) if side is None else (dquarter // 2, side * (dquarter // 2))
+        return w2_out.at[spot(owner * deep + part * dquarter + start, size, 16), :]
+
+    def whole(kind, owner):
+        if kind == "a":
+            return a_full.at[spot(owner * share, share, 16), :]
+        if kind == "e":
+            return e_out.at[spot(owner * share, share, 16), :]
+        if kind == "w":
+            return w2_out.at[spot(owner * deep, deep, 16), :]
+        return v_all.at[owner]
+
+    def own(kind):
+        return {"a": whole("a", me), "e": e_own, "w": w2_own, "v": v_all.at[me]}[kind]
+
+    def own_quarter(kind):
+        if kind == "a":
+            return region("a", me, here.wide)
+        if kind == "e":
+            return e_own.at[:, spot(here.wide * equarter, equarter, LANES)]
+        return w2_own.at[spot(here.wide * dquarter, dquarter, 16), :]
+
+    def send_z(kind, k):
+        links.start((kind, "z", k), own_quarter(kind), region(kind, me, here.wide), here.z_dev(k))
+
+    def send_own(kind):
+        links.start((kind, "o"), own(kind), whole(kind, me), here.sib_dev)
+
+    def pass_z(kind, k):
+        piece = region(kind, here.behind(k), here.wide)
+        links.arrived((kind, "z", k), piece, here.z_dev(k))
+        links.start((kind, "x", k), piece, piece, here.x_dev)
+        links.start((kind, "y", k), piece, piece, here.y_dev)
+        links.start((kind, "sz", k), piece, piece, here.sib_dev)
+
+    def pass_xy(kind, k):
+        owner = here.behind(k)
+        piece = region(kind, owner, here.x_quarter)
+        links.arrived((kind, "x", k), piece, here.x_dev)
+        part = region(kind, owner, here.x_quarter, 0)
+        links.start((kind, "dy", k), part, part, here.y_dev)
+        links.start((kind, "sx", k), piece, piece, here.sib_dev)
+        piece = region(kind, owner, here.y_quarter)
+        links.arrived((kind, "y", k), piece, here.y_dev)
+        part = region(kind, owner, here.y_quarter, 1)
+        links.start((kind, "dx", k), part, part, here.x_dev)
+        links.start((kind, "sy", k), piece, piece, here.sib_dev)
+
+    def pass_d(kind, k):
+        owner = here.behind(k)
+        links.arrived((kind, "dy", k), region(kind, owner, here.d_quarter, 0), here.y_dev)
+        links.arrived((kind, "dx", k), region(kind, owner, here.d_quarter, 1), here.x_dev)
+        piece = region(kind, owner, here.d_quarter)
+        links.start((kind, "sd", k), piece, piece, here.sib_dev)
+
+    def from_sib(kind, way, part):
+        for k in steps:
+            links.arrived((kind, way, k), region(kind, here.behind(k, True), part), here.sib_dev)
+
+    low = low_lanes(share)
+    for pair in range(heads // 2):
+        tiles = [proj_ref[:, slice(b * width + pair * LANES, b * width + (pair + 1) * LANES)] for b in range(6)]
+        turned = [swap_halves(tile) for tile in tiles]
+        for odd in range(2):
+            for b in range(3):
+                left, right = (turned[2 * b], tiles[2 * b + 1]) if odd else (tiles[2 * b], turned[2 * b + 1])
+                at = (2 * pair + odd) * GROUP + b * LANES
+                a_full[spot(me * share, share, 16), at : at + LANES] = jnp.where(low, left, right).astype(BF16)
+    v_all[me] = jnp.zeros_like(v_all[me])
+    v_all[me, 0 : vec_ref.shape[0], 0 : vec_ref.shape[1]] = vec_ref[...].astype(BF16)
+
+    here.greet()
+    for k in steps:
+        send_z("a", k)
+        links.start(("v", "z", k), v_all.at[me], v_all.at[me], here.z_dev(k))
+    send_own("v")
+    send_own("a")
+
+    inner = w1_ref.shape[1]
+    e_own[:, 0:inner] = w1_ref[...].astype(BF16)
+    e_own[:, inner : inner + width] = wo_ref[...].astype(BF16)
+    e_own[:, inner + width :] = jnp.zeros((share, e_own.shape[1] - inner - width), BF16)
+    w2_own[...] = w2_ref[...].astype(BF16)
+    copy_e = pltpu.make_async_copy(e_own, whole("e", me), local.at[0])
+    copy_w = pltpu.make_async_copy(w2_own, whole("w", me), local.at[1])
+    copy_e.start()
+    copy_w.start()
+
+    for k in steps:
+        pass_z("a", k)
+        send_z("e", k)
+        owner = here.behind(k)
+        links.arrived(("v", "z", k), v_all.at[owner], here.z_dev(k))
+        links.start(("v", "sz", k), v_all.at[owner], v_all.at[owner], here.sib_dev)
+    for k in steps:
+        pass_xy("a", k)
+    send_own("e")
+    send_own("w")
+
+    links.arrived(("v", "o"), v_all.at[here.sib], here.sib_dev)
+    for k in steps:
+        owner = here.behind(k, True)
+        links.arrived(("v", "sz", k), v_all.at[owner], here.sib_dev)
+    span = vec_ref.shape[1]
+    vec_out[...] = jnp.concatenate([v_all[n].astype(F32)[:, 0:span] for n in range(narrow)], axis=1)
+    low1 = low_lanes(1)
+    for head in range(heads):
+        cols = slice((head // 2) * LANES, (head // 2 + 1) * LANES)
+        row = [vec_out[r : r + 1, cols] for r in range(4)] + [jnp.zeros((1, LANES), F32), vec_out[4:5, cols]]
+        for b in range(3):
+            left, right = row[2 * b], row[2 * b + 1]
+            left, right = (swap_halves(left), right) if head % 2 else (left, swap_halves(right))
+            at = head * GROUP + b * LANES
+            bias[0:1, at : at + LANES] = jnp.where(low1, left, right)
+
+    links.arrived(("a", "o"), whole("a", here.sib), here.sib_dev)
+    outs = []
+
+    def project(index, part):
+        size = 256
+        cols = spot(part * quarter, quarter, LANES)
+        add = bias[0:1, cols]
+
+        def tile(i, carry):
+            at = spot(i * size, size, size)
+            prod = mm(x_ref[at, :], a_full[:, cols])
+            word = word_ref[at, :] > 0
+            for head in range(quarter // GROUP):
+                group = slice(head * GROUP, (head + 1) * GROUP)
+                out = slice(head * LANES, (head + 1) * LANES)
+                query, keyval = qkv_tile(prod[:, group], add[:, group], word)
+                q_s[index, at, out] = query
+                kv_s[index, at, out] = keyval
+            return carry
+
+        lax.fori_loop(0, rows // size, tile, 0)
+        wide = q_s.shape[2]
+        for number, (source, target) in enumerate(((q_s, q_out), (kv_s, kv_out))):
+            copy = pltpu.make_async_copy(
+                source.at[index], target.at[:, spot(part * wide, wide, LANES)], local.at[2 + 2 * index + number]
+            )
+            copy.start()
+            outs.append(copy)
+
+    from_sib("a", "sz", here.wide)
+    project(0, here.wide)
+    for k in steps:
+        pass_z("e", k)
+        send_z("w", k)
+    for k in steps:
+        pass_d("a", k)
+    from_sib("a", "sx", here.x_quarter)
+    project(1, here.x_quarter)
+    for k in steps:
+        pass_xy("e", k)
+    from_sib("a", "sy", here.y_quarter)
+    project(2, here.y_quarter)
+    from_sib("a", "sd", here.d_quarter)
+    project(3, here.d_quarter)
+    copy_a = pltpu.make_async_copy(a_full, a_out, local.at[10])
+    copy_a.start()
+    for k in steps:
+        pass_z("w", k)
+    for k in steps:
+        pass_d("e", k)
+    for k in steps:
+        pass_xy("w", k)
+    for k in steps:
+        pass_d("w", k)
+    for kind in ("e", "w"):
+        links.arrived((kind, "o"), whole(kind, here.sib), here.sib_dev)
+        for way, part in (("sz", here.wide), ("sx", here.x_quarter), ("sy", here.y_quarter), ("sd", here.d_quarter)):
+            from_sib(kind, way, part)
+    links.finish()
+    for copy in (copy_e, copy_w, copy_a, *outs):
+        copy.wait()
+
+
+def gather_call(narrow, x, proj, wo, w1, w2, vec, word):
+    rows, width = x.shape
+    share, deep, inner = proj.shape[0], w2.shape[0], w1.shape[1]
+    ecols = inner + width + 2 * LANES
+    heads = width // HEAD
+    depth = narrow // 2
+    count = 3 * (1 + 9 * (depth - 1)) + 1 + 2 * (depth - 1)
+    vmem = pl.BlockSpec(memory_space=pltpu.VMEM)
+    hbm = pl.BlockSpec(memory_space=pl.ANY)
+    shape = jax.ShapeDtypeStruct
+    part = heads // 4 * LANES
+    return pl.pallas_call(
+        functools.partial(gather_kernel, narrow),
+        in_specs=[vmem] * 7,
+        out_specs=[hbm] * 5 + [vmem],
+        out_shape=[
+            shape((rows, heads * LANES), BF16),
+            shape((rows, heads * LANES), BF16),
+            shape((width, proj.shape[1]), BF16),
+            shape((width, ecols), BF16),
+            shape((deep * narrow, width), BF16),
+            shape((16, width), F32),
+        ],
+        scratch_shapes=[
+            pltpu.VMEM((width, proj.shape[1]), BF16),
+            pltpu.VMEM((share, ecols), BF16),
+            pltpu.VMEM((deep, width), BF16),
+            pltpu.VMEM((narrow, 16, LANES), BF16),
+            pltpu.VMEM((8, proj.shape[1]), F32),
+            pltpu.VMEM((4, rows, part), BF16),
+            pltpu.VMEM((4, rows, part), BF16),
+            pltpu.SemaphoreType.DMA((count,)),
+            pltpu.SemaphoreType.DMA((count,)),
+            pltpu.SemaphoreType.DMA((11,)),
+        ],
+        compiler_params=pltpu.CompilerParams(
+            vmem_limit_bytes=VMEM_LIMIT, collective_id=0, has_side_effects=True
+        ),
+        name="gather",
+    )(x, proj, wo, w1, w2, vec, word)
 
 
 def key_pair(keyval, kmask, low):
@@ -235,7 +547,7 @@
 
 
 def middle_kernel(
-    tiles, x_ref, ctx_ref, cot_ref, vec_ref, wo_hbm, w1_hbm, w2_hbm,
+    tiles, x_ref, ctx_ref, cot_ref, vec_ref, e_hbm, w2_hbm,
     out_ref, gr1_ref, gctx_ref, gw2_ref, gw1_ref, gwo_ref, gvec_ref,
     wo, w1, w2, h1_s, act_s, gb_s, gp_s, ga_s, ctx_s, dg_s, acc, sems,
 ):
@@ -244,17 +556,18 @@
     inner = w1.shape[1]
     chunks = inner // width
 
-    def weight_copies():
-        return (
-            pltpu.make_async_copy(wo_hbm, wo, sems.at[0]),
-            pltpu.make_async_copy(w1_hbm, w1, sems.at[1]),
-            pltpu.make_async_copy(w2_hbm, w2, sems.at[2]),
-        )
+    def weight_copies(index):
+        source, target = (
+            (e_hbm.at[:, inner : inner + width], wo),
+            (e_hbm.at[:, 0:inner], w1),
+            (w2_hbm, w2),
+        )[index]
+        return pltpu.make_async_copy(source, target, sems.at[index])
 
     @pl.when(step == 0)
     def _():
-        for copy in weight_copies():
-            copy.start()
+        for index in range(3):
+            weight_copies(index).start()
         acc[...] = jnp.zeros_like(acc)
 
     def vec(row):
@@ -266,7 +579,7 @@
 
         @pl.when(step == 0)
         def _():
-            weight_copies()[0].wait()
+            weight_copies(0).wait()
 
         ctx_s[here, :] = ctx_ref[...]
         resid = x_ref[...].astype(F32) + mm(ctx_ref[...], wo[...]) + vec(5)
@@ -279,8 +592,8 @@
 
         @pl.when(step == 0)
         def _():
-            weight_copies()[1].wait()
-            weight_copies()[2].wait()
+            weight_copies(1).wait()
+            weight_copies(2).wait()
 
         branch = h1 + vec(8)
         for c in range(chunks):
@@ -346,9 +659,9 @@
             gvec_ref[row : row + 1, :] = jnp.sum(acc[row], axis=0, keepdims=True)
 
 
-def middle_call(x, ctx, cot, vec, wo, w1, w2, size):
+def middle_call(x, ctx, cot, vec, e, w2, size):
     rows, width = x.shape
-    inner = w1.shape[1]
+    inner = w2.shape[0]
     tiles, chunks = rows // size, inner // width
     tile = pl.BlockSpec((size, width), lambda i: (jnp.minimum(i, tiles - 1), 0))
     hbm = pl.BlockSpec(memory_space=pl.ANY)
@@ -360,7 +673,7 @@
     return pl.pallas_call(
         functools.partial(middle_kernel, tiles),
         grid=(tiles + 2 * chunks + 1,),
-        in_specs=[tile, tile, tile, pl.BlockSpec(vec.shape, lambda i: (0, 0)), hbm, hbm, hbm],
+        in_specs=[tile, tile, tile, pl.BlockSpec(vec.shape, lambda i: (0, 0)), hbm, hbm],
         out_specs=[
             tile,
             tile,
@@ -395,7 +708,7 @@
         ],
         compiler_params=pltpu.CompilerParams(vmem_limit_bytes=VMEM_LIMIT),
         name="middle",
-    )(x, ctx, cot, vec, wo, w1, w2)
+    )(x, ctx, cot, vec, e, w2)
 
 
 def input_grad_kernel(gp_ref, w_ref, gr1_ref, out_ref):
@@ -445,6 +758,11 @@
     return array_in.reshape(rows, heads, 6, HEAD).transpose(0, 2, 1, 3).reshape(rows, cols)
 
 
+def can_pass_pieces(wide, narrow, width, deep):
+    share = width // narrow
+    return wide == 4 and narrow % 2 == 0 and narrow > 2 and share % 32 == 0 and deep % 128 == 0
+
+
 def body(
     x_in, cotangent, segment_ids, type_ids,
     projection, context_out, expand_weight, reduce_weight, vector_params,
@@ -456,10 +774,6 @@
 
     def gather(array_in, axis):
         return lax.all_gather(array_in.astype(BF16), "narrow", axis=axis, tiled=True)
-
-    proj_w = gather(by_head(projection), 0)
-    vec_half = gather(vector_params, 1)
-    ctx_w, expand_w, reduce_w = gather(context_out, 0), gather(expand_weight, 0), gather(reduce_weight, 0)
 
     hidden = x_in.reshape(rows, width)
     cot = cotangent.reshape(rows, width)
@@ -471,20 +785,31 @@
     qaug = jnp.where(same & (lane < 8), 1.0, 0.0).astype(BF16)
     kaug = jnp.where(lane < 8, jnp.where(same, 0.0, FAR), jnp.where(lane < 11, 1.0, 0.0)).astype(BF16)
 
-    zero_row = jnp.zeros((1, width), BF16)
-    bias = by_head(jnp.concatenate([vec_half[0:4], zero_row, vec_half[4:5]]).reshape(1, -1)).astype(F32)
-
-    query, keyval = qkv_call(hidden, proj_w, bias, word)
+    narrow = lax.axis_size("narrow")
+    if can_pass_pieces(lax.axis_size("wide"), narrow, width, reduce_weight.shape[0]):
+        query, keyval, proj_w, mid_w, reduce_w, vec_rows = gather_call(
+            narrow, hidden, projection, context_out, expand_weight, reduce_weight, vector_params, word
+        )
+    else:
+        proj_w, vec_half = gather(by_head(projection), 0), gather(vector_params, 1)
+        reduce_w = gather(reduce_weight, 0)
+        mid_w = jnp.concatenate(
+            [gather(expand_weight, 0), gather(context_out, 0), jnp.zeros((width, 2 * LANES), BF16)], axis=1
+        )
+        zero_row = jnp.zeros((1, width), BF16)
+        bias = by_head(jnp.concatenate([vec_half[0:4], zero_row, vec_half[4:5]]).reshape(1, -1)).astype(F32)
+        vec_rows = jnp.pad(vec_half.astype(F32), ((0, 1), (0, 0)))
+        query, keyval = qkv_call(hidden, proj_w, bias, word)
     context, aug = attend_call(query, keyval, qaug, kaug, kmask, seq_len)
     block_out, grad_r1, grad_context, grad_reduce, grad_expand, grad_ctx_w, grad_mid = middle_call(
-        hidden, context, cot, vec_half, ctx_w, expand_w, reduce_w, 256
+        hidden, context, cot, vec_rows, mid_w, reduce_w, 256
     )
     grad_proj, grad_proj_w, grad_sums = attend_back_call(
         hidden, query, keyval, aug, grad_context, context, kaug, kmask, word, seq_len
     )
     input_grad = input_grad_call(grad_proj, proj_w, grad_r1, 256)
     sum_rows = by_block(grad_sums).reshape(6, width)
-    grad_vectors = jnp.concatenate([sum_rows[0:4], sum_rows[5:6], grad_mid[5:]], axis=0)
+    grad_vectors = jnp.concatenate([sum_rows[0:4], sum_rows[5:6], grad_mid[5:15]], axis=0)
 
     def scatter(array_in, axis):
         return lax.psum_scatter(array_in, "narrow", scatter_dimension=axis, tiled=True)

time: 710 us -> 625 us (0.88)
  waiting for transfers between devices: 392 us -> 265 us
  Pallas kernels: 188 us -> 253 us
  blocking collectives: 42.7 us -> 26.9 us
    all_gather x4 -> x0, waiting for transfers between devices: 134 us -> none  [gather(): lax.all_gather(array_in.astype(BF16), 'narrow', axis=axis, tiled=True)]
    pallas_call x1, Pallas kernels: 16.7 us -> 81 us  [gather_call(): pl.pallas_call(functools.partial(gather_kernel, narrow), in_specs=[vmem]...]
    all_gather x1 -> x0, blocking collectives: 15.8 us -> none  [gather(): lax.all_gather(array_in.astype(BF16), 'narrow', axis=axis, tiled=True)]
    reduce_scatter x4, waiting for transfers between devices: 168 us -> 177 us  [scatter(): lax.psum_scatter(array_in, 'narrow', scatter_dimension=axis, tiled=True)]
    unnamed x11 -> x7, waiting for transfers between devices: 27.2 us -> 25.2 us
    unnamed x54 -> x49, local copies, waits for them, and re-layouts: 20.8 us -> 20.7 us
  transfers between devices with their start and end apart: 10 -> 6, of which waited for: 8 -> 5; matrix products, arithmetic and copies ran while one was open for 3% -> 2% of each run, Pallas kernels for 13% -> 8%
where the time goes in v2:
time: 625 us; the launch traced here: 617 us
  waiting for transfers between devices  265 us (42%)
  Pallas kernels  253 us (40%)
  local copies, waits for them, and re-layouts  27.6 us (4%)
  blocking collectives  26.9 us (4%)
  other arithmetic  24.3 us (4%)
  between operations  19.7 us (3%)
    reduce_scatter x4, waiting for transfers between devices, scatter(): lax.psum_scatter(array_in, 'narrow', scatter_dimension=axis, tiled=True)  177 us
    pallas_call x1, Pallas kernels, gather_call(): pl.pallas_call(functools.partial(gather_kernel, narrow), in_specs=[vmem]...  81 us
    pallas_call x1, Pallas kernels, middle_call(): pl.pallas_call(functools.partial(middle_kernel, tiles), grid=(tiles + 2 *...  80.8 us
    psum x1, waiting for transfers between devices, over_wide(): return lax.psum(array_in.astype(BF16), 'wide').astype(F32)  62.7 us
    pallas_call x1, Pallas kernels, attend_back_call(): pl.pallas_call(functools.partial(attend_back_kernel, length), grid=(heads...  48.9 us
    pallas_call x1, Pallas kernels, attend_call(): pl.pallas_call(attend_kernel, grid=(seqs, steps), in_specs=[pair, pair, o...  26.4 us
    unnamed x7, waiting for transfers between devices  25.2 us
    unnamed x49, local copies, waits for them, and re-layouts  20.7 us
  transfers between devices with their start and end apart: 6, of which 5 were waited for; matrix products, arithmetic and copies ran while one was open for 2% of the time, Pallas kernels for 8%

profile of v2, /device:TPU:0, one launch (start us, length us, event | category | flops | bytes accessed | tf_op | source)
XLA Modules:
  0.0 616.7 jit_solution(8669754672991824470)
XLA Ops:
  7.2 0.0 reduce-scatter.10.cloned.1.call-start
  7.3 0.7 broadcast_compare_fusion
  8.0 0.7 eq.24
  8.7 1.0 compare_convert_fusion.km_ref
  9.7 1.0 select_convert_fusion.1.qa_ref
  10.6 1.0 select_convert_fusion.ka_ref
  11.6 1.0 broadcast_in_dim.28.word_ref
  12.5 81.0 %gather.1 = (bf16[1280,1536]{1,0:T(8,128)(2,1)}, bf16[1280,1536]{1,0:T(8,128)(2,1)}, bf16[768,4608]{1,0:T(8,128)(2,1)}, bf16[768,4096]{1,0:T(8,128)(2,1)}, bf16[3072,768]{1,0:T(8,128)(2,1)}, /*index=5*/f32[16,768]{1,0:T(8,128)}) custom-call(bf16[1280,768]{1,0:T(8,128)(2,1)} %bitcast.17, f32[96,4608]{1,0:T(8,128)} %proj_ref.1, f32[96,768]{1,0:T(8,128)} %wo_ref.1, ...), custom_call_target="tpu_custom_call" | custom-call | tf_op jit(solution)/shard_map/gather/pallas_call | solution.py:376
  93.6 26.4 %attend.1 = (bf16[1280,768]{1,0:T(8,128)(2,1)}, bf16[1280,1536]{1,0:T(8,128)(2,1)}) custom-call(bf16[1280,1536]{1,0:T(8,128)(2,1)} %get-tuple-element.41.q_ref, bf16[1280,1536]{1,0:T(8,128)(2,1)} %get-tuple-element.42.kv_ref, bf16[1280,128]{1,0:T(8,128)(2,1)} %select_convert_fusion.1.qa_ref, bf16[1280,128]{1,0:T(8,128)(2,1)} %select_convert_fusion.ka_ref, ...), custom_call_target="tpu_custom_call" | custom-call | tf_op jit(solution)/shard_map/attend/pallas_call | solution.py:441
  120.0 80.8 %middle.1 = (bf16[1280,768]{1,0:T(8,128)(2,1)}, f32[1280,768]{1,0:T(8,128)}, bf16[1280,768]{1,0:T(8,128)(2,1)}, bf16[3072,768]{1,0:T(8,128)(2,1)}, bf16[768,3072...) custom-call(bf16[1280,768]{1,0:T(8,128)(2,1)} %bitcast.18, ...), custom_call_target="tpu_custom_call" | custom-call | tf_op jit(solution)/shard_map/middle/pallas_call | solution.py:673
  200.8 0.0 reduce-scatter.10.cloned.1.call-update
  200.8 0.0 reduce-scatter.12.cloned.1.call-start
  200.8 0.7 reduce-scatter.12.cloned.1.call-update
  201.5 0.0 reduce-scatter.14.cloned.1.call-start
  201.6 0.7 reduce-scatter.14.cloned.1.call-update
  202.3 0.0 reduce-scatter.8.cloned.1.call-start
  202.3 48.9 %attend_back.1 = (bf16[1280,4608]{1,0:T(8,128)(2,1)}, bf16[768,4608]{1,0:T(8,128)(2,1)}, f32[1,4608]{1,0:T(1,128)}) custom-call(bf16[1280,768]{1,0:T(8,128)(2,1)} %bitcast.19, bf16[1280,1536]{1,0:T(8,128)(2,1)} %get-tuple-element.41.q_ref, bf16[1280,1536]{1,0:T(8,128)(2,1)} %get-tuple-element.42.kv_ref, bf16[1280,1536]{1,0:T(8,128)(2,1)} %get-tuple-element.48.aug_ref, ...), custom_call_target="tpu_custom_call" | custom-call | tf_op jit(solution)/shard_map/attend_back/pallas_call | solution.py:514
  251.3 0.0 copy-start.17
  251.3 0.0 reduce-scatter.8.cloned.1.call-update
  251.3 0.0 reduce-scatter.16.cloned.1.call-start
  251.3 0.7 copy-done.15
  252.1 0.1 reshape.78
  252.2 0.1 slice.18
  252.3 0.1 slice.16
  252.4 0.9 copy.66
  253.4 0.0 reduce-scatter.16.cloned.1.call-update
  253.4 0.0 all-reduce.3.cloned.1.call-start
  253.4 0.0 reduce-scatter.10.cloned.1.call-done
  253.5 43.9 %reduce-scatter.12.cloned.1.call-done = bf16[96,3072]{1,0:T(8,128)(2,1)} async-done(((bf16[768,3072]{1,0:T(8,128)(2,1)}), bf16[96,3072]{1,0:T(8,128)(2,1)}) %reduce-scatter.12.cloned.1.call-update) | async-done | bytes 589840 | tf_op jit(solution)/shard_map/reduce_scatter | solution.py:815
  297.3 55.6 %reduce-scatter.14.cloned.1.call-done = bf16[384,768]{1,0:T(8,128)(2,1)} async-done(((bf16[3072,768]{1,0:T(8,128)(2,1)}), bf16[384,768]{1,0:T(8,128)(2,1)}) %reduce-scatter.14.cloned.1.call-update) | async-done | bytes 589840 | tf_op jit(solution)/shard_map/reduce_scatter | solution.py:815
  353.0 77.8 %reduce-scatter.8.cloned.1.call-done = bf16[96,4608]{1,0:T(8,128)(2,1)} async-done(((bf16[768,4608]{1,0:T(8,128)(2,1)}), bf16[96,4608]{1,0:T(8,128)(2,1)}) %reduce-scatter.8.cloned.1.call-update) | async-done | bytes 884752 | tf_op jit(solution)/shard_map/reduce_scatter | solution.py:815
  430.7 0.0 all-reduce.3.cloned.1.call-update
  430.8 1.9 copy.61
  432.7 3.0 copy.56
  435.7 3.0 copy.59
  438.7 23.8 %reduce-scatter.16.cloned.1.call-done = f32[96,15]{1,0:T(8,128)} async-done(((f32[768,15]{1,0:T(8,128)}), f32[96,15]{1,0:T(8,128)}) %reduce-scatter.16.cloned.1.call-update) | async-done | bytes 5776
  462.5 0.9 copy.67
  463.3 10.0 %psum.46 = bf16[15,96]{1,0:T(8,128)(2,1)S(1)} all-reduce(bf16[15,96]{1,0:T(8,128)(2,1)S(1)} %copy.67), channel_id=1, replica_groups=mesh['wide'=4,'narrow'=8] {'wide'}, use_global_device_ids=true, to_apply=%region_13.14 | all-reduce | flops 1440 | bytes 5760 | tf_op jit(solution)/shard_map/psum | solution.py:818
  473.3 0.6 fusion.18
  473.9 62.7 %all-reduce.3.cloned.1.call-done = (bf16[96,4608]{1,0:T(8,128)(2,1)}, bf16[96,768]{1,0:T(8,128)(2,1)}, bf16[96,3072]{1,0:T(8,128)(2,1)}, bf16[384,768]{1,0:T(8,128)(2,1)}) async-done(((bf16[96,4608]{1,0:T(8,128)(2,1)}, bf16[96,768]{1,0:T(8,128)(2,1)}, bf16[96,3072]{1,0:T(8,128)(2,1)}, bf16[384,768]{1,0:T(8,128)(2,1)}), (bf16[96,4608]{1,0:T(8,128)(2,1)}, bf16[96,768]{1,0:T(8,128)(2,1)}, ...) | async-done | bytes 2211856 | tf_op jit(solution)/shard_map/psum | solution.py:818
  536.6 2.1 fusion.8
  538.7 2.0 fusion.7
  540.7 0.7 fusion.14
  541.3 1.1 fusion.2
  545.6 15.6 %input_grad.1 = bf16[1280,768]{1,0:T(8,128)(2,1)} custom-call(bf16[1280,4608]{1,0:T(8,128)(2,1)} %get-tuple-element.50.gp_ref, bf16[768,4608]{1,0:T(8,128)(2,1)} %get-tuple-element.51.w_ref, f32[1280,768]{1,0:T(8,128)} %get-tuple-element.52.gr1_ref), custom_call_target="tpu_custom_call" | custom-call | tf_op jit(solution)/shard_map/input_grad/pallas_call | solution.py:721
  561.3 16.9 %psum.47 = f32[]{:T(128)} all-reduce(f32[]{:T(128)S(6)} %add.115), channel_id=1, replica_groups=mesh['wide'=4,'narrow'=8] {'narrow'}, use_global_device_ids=true, to_apply=%region_15.16 | all-reduce | flops 1 | bytes 8 | tf_op jit(solution)/shard_map/psum | solution.py:831
  578.9 1.4 convert_multiply_fusion
  580.2 3.0 copy.57
  583.2 2.0 copy.58
  585.2 0.4 copy-done
  585.6 0.7 copy-done.1
  586.3 4.2 fusion.32
  590.5 1.3 copy.65
  591.8 2.9 copy.62
  594.7 3.1 copy.63
  597.8 0.0 copy-start.19
  597.8 0.0 copy-start.8
  597.8 1.8 copy.64
  599.7 0.6 fusion.20
  600.3 1.1 fusion.29
  601.5 0.0 copy-start.9
  601.5 0.0 copy-start.10
  601.5 4.4 fusion.23
  605.9 2.6 fusion.26
  (43 shorter events, 0.2 us)
Async XLA Ops:
  7.2 246.3 %reduce-scatter.10.cloned.1.call-start = ((), (), s32[]{:S(2)}) async-start(), calls=%async_computation.6 | async-start | bytes 1327104 | tf_op jit(solution)/shard_map/reduce_scatter | solution.py:815
  200.8 96.5 %reduce-scatter.12.cloned.1.call-start = ((), (), s32[]{:S(2)}) async-start(), calls=%async_computation.7 | async-start | bytes 5308416 | tf_op jit(solution)/shard_map/reduce_scatter | solution.py:815
  201.5 151.4 %reduce-scatter.14.cloned.1.call-start = ((), (), s32[]{:S(2)}) async-start(), calls=%async_computation.8 | async-start | bytes 5308416 | tf_op jit(solution)/shard_map/reduce_scatter | solution.py:815
  202.3 228.5 %reduce-scatter.8.cloned.1.call-start = ((), (), s32[]{:S(2)}) async-start(), calls=%async_computation.5 | async-start | bytes 7962624 | tf_op jit(solution)/shard_map/reduce_scatter | solution.py:815
  251.3 0.8 copy-start.15
  251.3 0.8 copy-start.17
  251.3 211.2 %reduce-scatter.16.cloned.1.call-start = ((), (), s32[]{:S(2)}) async-start(), calls=%async_computation.9 | async-start | bytes 442368
  253.4 283.2 %all-reduce.3.cloned.1.call-start = ((), (), s32[]{:S(2)}) async-start(), calls=%async_computation.10 | async-start | bytes 4423680 | tf_op jit(solution)/shard_map/psum | solution.py:818
  536.6 4.0 copy-start.11
  536.6 4.7 copy-start.5
  583.2 2.4 copy-start
  583.2 3.1 copy-start.1
  594.7 3.1 copy-start.2
  597.8 1.9 copy-start.16
  597.8 1.9 copy-start.18
  597.8 1.9 copy-start.19
  597.8 2.5 copy-start.8
  597.8 2.5 copy-start.12
  597.8 2.5 copy-start.13
  597.8 2.5 copy-start.14
  599.7 1.8 copy-start.3
  599.7 1.8 copy-start.7
  601.5 4.4 copy-start.4
  601.5 4.4 copy-start.6
  601.5 4.4 copy-start.9
  601.5 4.4 copy-start.10
Sparse Core Ops, SparseCore 0:
  200.9 40.9 reduce-scatter.9
  244.2 53.0 reduce-scatter.11
  299.6 53.2 reduce-scatter.13
  355.1 75.5 reduce-scatter.7
  433.4 28.9 reduce-scatter.15
  466.2 70.3 all-reduce.2
